TPU v7x, 512 devices: a whole 4x4x16 slice. The times are simulated.
512 devices in a mesh: dp: 8 (over x, core), row: 8 (over y, z_hi), col: 8 (over z_lo).
Axes of the slice: x: 4, y: 4, z: 16 (z_hi: 2, z_lo: 8; z = z_hi * 8 + z_lo), core: 2. Of those that a mesh axis runs over, the one named last changes fastest.
Arguments:
- activations: bfloat16 [384, 8192], P(('dp', 'col'), 'row'), may hold values from -6 to 6
- gate_weight: bfloat16 [8192, 24576], P('row', ('dp', 'col')), may hold values from -0.0625 to 0.0625
- up_weight: bfloat16 [8192, 24576], P('row', ('dp', 'col')), may hold values from -0.0625 to 0.0625
- down_weight: bfloat16 [24576, 8192], P(('dp', 'col'), 'row'), may hold values from -0.0390625 to 0.0390625
- output_cotangent: bfloat16 [384, 8192], P(('dp', 'col'), 'row'), may hold values from -6 to 6
Outputs:
- layer_output: bfloat16 [384, 8192], P(('dp', 'col'), 'row')
- input_gradient: bfloat16 [384, 8192], P(('dp', 'col'), 'row')
- gate_gradient: bfloat16 [8192, 24576], P('row', ('dp', 'col'))
- up_gradient: bfloat16 [8192, 24576], P('row', ('dp', 'col'))
- down_gradient: bfloat16 [24576, 8192], P(('dp', 'col'), 'row')
All inputs are finite; a program needn't handle non-finite values.
Results may differ from a plain program's by a relative error of at most 0.029.
Values may be sent and summed in bfloat16 or wider, within the bound.
A program may use at most 64 MiB of HBM per device.

v0:
```python
import jax
import jax.numpy as jnp
from jax import lax
from jax.sharding import PartitionSpec as P


def contract_rows(left_side, right_side):
    return lax.dot_general(
        left_side, right_side, (((1,), (1,)), ((), ())), preferred_element_type=jnp.float32
    )


def contract_tokens(left_side, right_side):
    return lax.dot_general(
        left_side, right_side, (((0,), (0,)), ((), ())), preferred_element_type=jnp.float32
    )


def gated_hidden(gate_sum, up_sum):
    sigmoid = jax.nn.sigmoid(gate_sum)
    return (gate_sum * sigmoid * up_sum).astype(jnp.bfloat16)


def slope_pair(hidden_slope, gate_sum, up_sum):
    sigmoid = jax.nn.sigmoid(gate_sum)
    gate_slope = (hidden_slope * up_sum * sigmoid * (1.0 + gate_sum * (1.0 - sigmoid))).astype(
        jnp.bfloat16
    )
    up_slope = (hidden_slope * gate_sum * sigmoid).astype(jnp.bfloat16)
    return (gate_slope, up_slope)


def body(activations, gate_weight, up_weight, down_weight, output_cotangent):
    all_rows, all_cotangent = (
        lax.all_gather(activations, ("dp", "col"), axis=0, tiled=True),
        lax.all_gather(output_cotangent, ("dp", "col"), axis=0, tiled=True),
    )
    hidden_width = gate_weight.shape[1]
    both_sums = lax.psum_scatter(
        jnp.concatenate(
            [
                jnp.dot(all_rows, gate_weight, preferred_element_type=jnp.float32),
                jnp.dot(all_rows, up_weight, preferred_element_type=jnp.float32),
            ],
            axis=1,
        ).astype(jnp.bfloat16),
        "row",
        scatter_dimension=0,
        tiled=True,
    ).astype(jnp.float32)
    gate_sum = both_sums[:, :hidden_width]
    up_sum = both_sums[:, hidden_width:]
    hidden_rows = lax.all_gather(gated_hidden(gate_sum, up_sum), "row", axis=0, tiled=True)
    hidden_slope = lax.psum_scatter(
        contract_rows(all_cotangent, down_weight).astype(jnp.bfloat16),
        "row",
        scatter_dimension=0,
        tiled=True,
    ).astype(jnp.float32)
    gate_slope, up_slope = slope_pair(hidden_slope, gate_sum, up_sum)
    gate_all, up_all = (
        lax.all_gather(gate_slope, "row", axis=0, tiled=True),
        lax.all_gather(up_slope, "row", axis=0, tiled=True),
    )
    output_total = lax.psum_scatter(
        jnp.dot(hidden_rows, down_weight, preferred_element_type=jnp.float32),
        ("dp", "col"),
        scatter_dimension=0,
        tiled=True,
    )
    input_total = lax.psum_scatter(
        contract_rows(gate_all, gate_weight) + contract_rows(up_all, up_weight),
        ("dp", "col"),
        scatter_dimension=0,
        tiled=True,
    )
    gate_gradient = contract_tokens(all_rows, gate_all).astype(jnp.bfloat16)
    up_gradient = contract_tokens(all_rows, up_all).astype(jnp.bfloat16)
    down_gradient = contract_tokens(hidden_rows, all_cotangent).astype(jnp.bfloat16)
    return (
        output_total.astype(jnp.bfloat16),
        input_total.astype(jnp.bfloat16),
        gate_gradient,
        up_gradient,
        down_gradient,
    )


def solution(mesh):
    in_specs = (
        P(("dp", "col"), "row"),
        P("row", ("dp", "col")),
        P("row", ("dp", "col")),
        P(("dp", "col"), "row"),
        P(("dp", "col"), "row"),
    )
    out_specs = (
        P(("dp", "col"), "row"),
        P(("dp", "col"), "row"),
        P("row", ("dp", "col")),
        P("row", ("dp", "col")),
        P(("dp", "col"), "row"),
    )
    return jax.shard_map(body, mesh=mesh, in_specs=in_specs, out_specs=out_specs, check_vma=False)
```

profile of v0, /device:TPU:1, one launch (start us, length us, event | category | flops | bytes accessed | tf_op | source)
XLA Modules:
  0.0 1137.2 jit_solution(7137992364079298130)
XLA Ops:
  7.2 203.0 %all-gather = bf16[64,6,1024]{2,1,0:T(8,128)(2,1)S(1)} all-gather(bf16[1,6,1024]{2,1,0:T(8,128)(2,1)} %bitcast.32), channel_id=1, replica_groups=mesh['dp'=8,'row'=8,'col'=8] {'dp','col'}, dimensions={0}, use_global_device_ids=true | all-gather | bytes 798720 | tf_op jit(solution)/shard_map/all_gather | solution.py:35
  213.0 218.2 %all-gather.1 = bf16[64,6,1024]{2,1,0:T(8,128)(2,1)S(1)} all-gather(bf16[1,6,1024]{2,1,0:T(8,128)(2,1)S(1)} %bitcast.33), channel_id=1, replica_groups=mesh['dp'=8,'row'=8,'col'=8] {'dp','col'}, dimensions={0}, use_global_device_ids=true | all-gather | bytes 798720 | tf_op jit(solution)/shard_map/all_gather | solution.py:36
  431.5 2.7 convolution_convert_fusion.3
  435.2 129.5 %reduce-scatter.13.cloned.1.call-done = bf16[48,384]{1,0:T(8,128)(2,1)} async-done(((bf16[384,384]{1,0:T(8,128)(2,1)}), bf16[48,384]{1,0:T(8,128)(2,1)}) %reduce-scatter.13.cloned.1.call-update) | async-done | bytes 36880 | tf_op jit(solution)/shard_map/reduce_scatter | solution.py:54
  565.5 58.5 %all_gather.18 = bf16[384,384]{1,0:T(8,128)(2,1)S(1)} all-gather(bf16[48,384]{1,0:T(8,128)(2,1)S(1)} %get-tuple-element.30), channel_id=1, replica_groups=mesh['dp'=8,'row'=8,'col'=8] {'row'}, dimensions={0}, use_global_device_ids=true | all-gather | bytes 331776 | tf_op jit(solution)/shard_map/all_gather | solution.py:62
  624.6 58.9 %all_gather.19 = bf16[384,384]{1,0:T(8,128)(2,1)S(1)} all-gather(bf16[48,384]{1,0:T(8,128)(2,1)S(1)} %get-tuple-element.29), channel_id=1, replica_groups=mesh['dp'=8,'row'=8,'col'=8] {'row'}, dimensions={0}, use_global_device_ids=true | all-gather | bytes 331776 | tf_op jit(solution)/shard_map/all_gather | solution.py:63
  683.6 65.2 %all_gather.16 = bf16[384,384]{1,0:T(8,128)(2,1)S(1)} all-gather(bf16[48,384]{1,0:T(8,128)(2,1)S(1)} %get-tuple-element.31), channel_id=1, replica_groups=mesh['dp'=8,'row'=8,'col'=8] {'row'}, dimensions={0}, use_global_device_ids=true | all-gather | bytes 331776 | tf_op jit(solution)/shard_map/all_gather | solution.py:53
  749.5 1.7 fusion.12
  751.8 243.6 %fusion.9 = (f32[8,1024]{1,0:T(8,128)S(1)}, f32[8,1024]{1,0:T(8,128)S(1)}) fusion(f32[384,1024]{1,0:T(8,128)} %fusion.12, f32[384,1024]{1,0:T(8,128)S(1)} %convolution_add_fusion), kind=kCustom, calls=%all-reduce-scatter.2 | all-reduce-scatter fusion | flops 1048577 | bytes 3213312
  995.4 1.3 collective-permute-start.31
  996.8 1.3 collective-permute-start.15
  998.1 2.5 collective-permute-start.16
  1000.6 1.9 collective-permute-start.17
  1002.5 11.8 %collective-permute-start.18 = (bf16[8,1024]{1,0:T(8,128)(2,1)S(1)}, bf16[8,1024]{1,0:T(8,128)(2,1)S(1)}, u32[]{:S(2)}, u32[]{:S(2)}) collective-permute-start(bf16[8,1024]{1,0:T(8,128)(2,1)S(1)} %convert.70), channel_id=1, source_target_pairs={{0,3},{1,4},{2,5},{3,6},{4,7},{5,64},{6,65},{7,66},{64,67},{65,68}... | collective-permute-start | bytes 49160
  1014.3 13.3 %collective-permute-start.19 = (bf16[8,1024]{1,0:T(8,128)(2,1)S(1)}, bf16[8,1024]{1,0:T(8,128)(2,1)S(1)}, u32[]{:S(2)}, u32[]{:S(2)}) collective-permute-start(bf16[8,1024]{1,0:T(8,128)(2,1)S(1)} %convert.70), channel_id=1, source_target_pairs={{0,4},{1,5},{2,6},{3,7},{4,64},{5,65},{6,66},{7,67},{64,68},{65,69... | collective-permute-start | bytes 49160
  1027.7 10.9 collective-permute-start.20
  1038.6 3.9 collective-permute-start.21
  1042.5 9.0 collective-permute-start.22
  1051.5 1.9 collective-permute-start.23
  1053.5 1.7 collective-permute-start.24
  1055.2 3.2 collective-permute-start.25
  1058.4 1.3 dynamic-slice.6
  1060.4 2.8 collective-permute-start.26
  1063.2 6.9 collective-permute-start.27
  1070.2 1.9 collective-permute-start.28
  1072.1 1.3 collective-permute-start.29
  1074.1 2.6 collective-permute-start.30
  1076.8 1.6 fusion.2
  1078.9 1.9 collective-permute-start
  1080.9 1.9 collective-permute-start.1
  1082.8 2.4 collective-permute-start.10
  1085.2 3.1 collective-permute-start.11
  1088.9 7.0 collective-permute-start.12
  1096.6 1.3 collective-permute-start.13
  1097.9 2.0 collective-permute-start.14
  1099.9 1.9 collective-permute-start.2
  1101.9 3.7 collective-permute-start.3
  1105.6 3.7 collective-permute-start.4
  1109.4 1.5 convolution_convert_fusion
  1111.1 1.2 copy.25
  1112.2 1.2 copy.26
  1113.5 1.9 concatenate.6
  1115.4 4.5 collective-permute-start.5
  1120.0 2.2 collective-permute-start.6
  1122.2 1.9 collective-permute-start.7
  1124.1 1.3 collective-permute-start.8
  1125.4 1.3 collective-permute-start.9
  1127.8 1.9 concatenate.5
  (150 shorter events, 11.0 us)
Async XLA Ops:
  7.2 204.0 %copy-start = (bf16[1024,384]{1,0:T(8,128)(2,1)S(1)}, bf16[1024,384]{1,0:T(8,128)(2,1)}, u32[]{:S(2)}) copy-start(bf16[1024,384]{1,0:T(8,128)(2,1)} %param.6) | copy-start | bytes 2359300
  7.2 203.3 %copy-start.6 = (bf16[1024,384]{1,0:T(8,128)(2,1)S(1)}, bf16[1024,384]{1,0:T(8,128)(2,1)}, u32[]{:S(2)}) copy-start(bf16[1024,384]{1,0:T(8,128)(2,1)} %param.7) | copy-start | bytes 2359300
  7.2 427.1 %reduce-scatter.11.cloned.1.call-start = ((), (), s32[]{:S(2)}) async-start(), calls=%async_computation.2 | async-start | bytes 663552 | tf_op jit(solution)/shard_map/reduce_scatter | solution.py:39
  212.9 351.8 %reduce-scatter.13.cloned.1.call-start = ((), (), s32[]{:S(2)}) async-start(), calls=%async_computation.3 | async-start | bytes 331776 | tf_op jit(solution)/shard_map/reduce_scatter | solution.py:54
  431.5 193.1 %copy-start.1 = (bf16[384,1024]{1,0:T(8,128)(2,1)}, bf16[384,1024]{1,0:T(8,128)(2,1)S(1)}, u32[]{:S(2)}) copy-start(bf16[384,1024]{1,0:T(8,128)(2,1)S(1)} %reshape.13) | copy-start | bytes 2359300
  624.0 124.8 %copy-start.5 = (bf16[384,384]{1,0:T(8,128)(2,1)}, bf16[384,384]{1,0:T(8,128)(2,1)S(1)}, u32[]{:S(2)}) copy-start(bf16[384,384]{1,0:T(8,128)(2,1)S(1)} %all_gather.18) | copy-start | bytes 884740
  624.0 125.5 %copy-start.8 = (bf16[384,1024]{1,0:T(8,128)(2,1)S(1)}, bf16[384,1024]{1,0:T(8,128)(2,1)}, u32[]{:S(2)}) copy-start(bf16[384,1024]{1,0:T(8,128)(2,1)} %param.8) | copy-start | bytes 2359300
  683.5 67.7 %copy-start.7 = (bf16[1024,384]{1,0:T(8,128)(2,1)S(1)}, bf16[1024,384]{1,0:T(8,128)(2,1)}, u32[]{:S(2)}) copy-start(bf16[1024,384]{1,0:T(8,128)(2,1)} %param.7) | copy-start | bytes 2359300
  995.4 18.9 %collective-permute-start.31 = (bf16[6,1024]{1,0:T(8,128)(2,1)S(1)}, bf16[6,1024]{1,0:T(8,128)(2,1)S(1)}, u32[]{:S(2)}, u32[]{:S(2)}) collective-permute-start(bf16[6,1024]{1,0:T(8,128)(2,1)S(1)} %slice.11), channel_id=1, source_target_pairs={{0,128},{1,129},{2,130},{3,131},{4,132},{5,133},{6,134},{7,135},{6... | collective-permute-start | bytes 36872
  996.8 30.9 %collective-permute-start.15 = (bf16[6,1024]{1,0:T(8,128)(2,1)S(1)}, bf16[6,1024]{1,0:T(8,128)(2,1)S(1)}, u32[]{:S(2)}, u32[]{:S(2)}) collective-permute-start(bf16[6,1024]{1,0:T(8,128)(2,1)S(1)} %slice.10), channel_id=1, source_target_pairs={{0,128},{1,129},{2,130},{3,131},{4,132},{5,133},{6,134},{7,135},{6... | collective-permute-start | bytes 36872
  998.1 40.5 %collective-permute-start.16 = (bf16[8,1024]{1,0:T(8,128)(2,1)S(1)}, bf16[8,1024]{1,0:T(8,128)(2,1)S(1)}, u32[]{:S(2)}, u32[]{:S(2)}) collective-permute-start(bf16[8,1024]{1,0:T(8,128)(2,1)S(1)} %convert.70), channel_id=1, source_target_pairs={{0,1},{1,2},{2,3},{3,4},{4,5},{5,6},{6,7},{7,64},{64,65},{65,66},{... | collective-permute-start | bytes 49160
  1000.6 41.9 %collective-permute-start.17 = (bf16[8,1024]{1,0:T(8,128)(2,1)S(1)}, bf16[8,1024]{1,0:T(8,128)(2,1)S(1)}, u32[]{:S(2)}, u32[]{:S(2)}) collective-permute-start(bf16[8,1024]{1,0:T(8,128)(2,1)S(1)} %convert.70), channel_id=1, source_target_pairs={{0,2},{1,3},{2,4},{3,5},{4,6},{5,7},{6,64},{7,65},{64,66},{65,67},... | collective-permute-start | bytes 49160
  1002.5 49.0 %collective-permute-start.18 = (bf16[8,1024]{1,0:T(8,128)(2,1)S(1)}, bf16[8,1024]{1,0:T(8,128)(2,1)S(1)}, u32[]{:S(2)}, u32[]{:S(2)}) collective-permute-start(bf16[8,1024]{1,0:T(8,128)(2,1)S(1)} %convert.70), channel_id=1, source_target_pairs={{0,3},{1,4},{2,5},{3,6},{4,7},{5,64},{6,65},{7,66},{64,67},{65,68}... | collective-permute-start | bytes 49160
  1014.3 39.1 %collective-permute-start.19 = (bf16[8,1024]{1,0:T(8,128)(2,1)S(1)}, bf16[8,1024]{1,0:T(8,128)(2,1)S(1)}, u32[]{:S(2)}, u32[]{:S(2)}) collective-permute-start(bf16[8,1024]{1,0:T(8,128)(2,1)S(1)} %convert.70), channel_id=1, source_target_pairs={{0,4},{1,5},{2,6},{3,7},{4,64},{5,65},{6,66},{7,67},{64,68},{65,69... | collective-permute-start | bytes 49160
  1027.7 27.5 %collective-permute-start.20 = (bf16[8,1024]{1,0:T(8,128)(2,1)S(1)}, bf16[8,1024]{1,0:T(8,128)(2,1)S(1)}, u32[]{:S(2)}, u32[]{:S(2)}) collective-permute-start(bf16[8,1024]{1,0:T(8,128)(2,1)S(1)} %convert.70), channel_id=1, source_target_pairs={{0,5},{1,6},{2,7},{3,64},{4,65},{5,66},{6,67},{7,68},{64,69},{65,7... | collective-permute-start | bytes 49160
  1038.6 21.8 %collective-permute-start.21 = (bf16[8,1024]{1,0:T(8,128)(2,1)S(1)}, bf16[8,1024]{1,0:T(8,128)(2,1)S(1)}, u32[]{:S(2)}, u32[]{:S(2)}) collective-permute-start(bf16[8,1024]{1,0:T(8,128)(2,1)S(1)} %convert.70), channel_id=1, source_target_pairs={{0,6},{1,7},{2,64},{3,65},{4,66},{5,67},{6,68},{7,69},{64,70},{65,... | collective-permute-start | bytes 49160
  1042.5 30.9 %copy-start.10 = (bf16[8,1024]{1,0:T(8,128)(2,1)}, bf16[8,1024]{1,0:T(8,128)(2,1)S(1)}, u32[]{:S(2)}) copy-start(bf16[8,1024]{1,0:T(8,128)(2,1)S(1)} %collective-permute-done.17) | copy-start | bytes 49156
  1042.5 20.6 %collective-permute-start.22 = (bf16[8,1024]{1,0:T(8,128)(2,1)S(1)}, bf16[8,1024]{1,0:T(8,128)(2,1)S(1)}, u32[]{:S(2)}, u32[]{:S(2)}) collective-permute-start(bf16[8,1024]{1,0:T(8,128)(2,1)S(1)} %convert.70), channel_id=1, source_target_pairs={{0,7},{1,64},{2,65},{3,66},{4,67},{5,68},{6,69},{7,70},{64,71},{65... | collective-permute-start | bytes 49160
  1051.5 21.9 %copy-start.12 = (bf16[8,1024]{1,0:T(8,128)(2,1)}, bf16[8,1024]{1,0:T(8,128)(2,1)S(1)}, u32[]{:S(2)}) copy-start(bf16[8,1024]{1,0:T(8,128)(2,1)S(1)} %collective-permute-done.18) | copy-start | bytes 49156
  1051.5 18.6 %collective-permute-start.23 = (bf16[8,1024]{1,0:T(8,128)(2,1)S(1)}, bf16[8,1024]{1,0:T(8,128)(2,1)S(1)}, u32[]{:S(2)}, u32[]{:S(2)}) collective-permute-start(bf16[8,1024]{1,0:T(8,128)(2,1)S(1)} %convert.70), channel_id=1, source_target_pairs={{0,64},{1,65},{2,66},{3,67},{4,68},{5,69},{6,70},{7,71},{64,128},{... | collective-permute-start | bytes 49160
  1053.5 20.0 %copy-start.14 = (bf16[8,1024]{1,0:T(8,128)(2,1)}, bf16[8,1024]{1,0:T(8,128)(2,1)S(1)}, u32[]{:S(2)}) copy-start(bf16[8,1024]{1,0:T(8,128)(2,1)S(1)} %collective-permute-done.19) | copy-start | bytes 49156
  1053.5 18.6 %collective-permute-start.24 = (bf16[8,1024]{1,0:T(8,128)(2,1)S(1)}, bf16[8,1024]{1,0:T(8,128)(2,1)S(1)}, u32[]{:S(2)}, u32[]{:S(2)}) collective-permute-start(bf16[8,1024]{1,0:T(8,128)(2,1)S(1)} %convert.70), channel_id=1, source_target_pairs={{0,65},{1,66},{2,67},{3,68},{4,69},{5,70},{6,71},{7,128},{64,129},... | collective-permute-start | bytes 49160
  1055.2 18.3 %copy-start.16 = (bf16[8,1024]{1,0:T(8,128)(2,1)}, bf16[8,1024]{1,0:T(8,128)(2,1)S(1)}, u32[]{:S(2)}) copy-start(bf16[8,1024]{1,0:T(8,128)(2,1)S(1)} %collective-permute-done.20) | copy-start | bytes 49156
  1055.2 18.2 %collective-permute-start.25 = (bf16[8,1024]{1,0:T(8,128)(2,1)S(1)}, bf16[8,1024]{1,0:T(8,128)(2,1)S(1)}, u32[]{:S(2)}, u32[]{:S(2)}) collective-permute-start(bf16[8,1024]{1,0:T(8,128)(2,1)S(1)} %convert.70), channel_id=1, source_target_pairs={{0,66},{1,67},{2,68},{3,69},{4,70},{5,71},{6,128},{7,129},{64,130}... | collective-permute-start | bytes 49160
  1060.3 49.1 %copy-start.2 = (bf16[384,1024]{1,0:T(8,128)(2,1)S(1)}, bf16[384,1024]{1,0:T(8,128)(2,1)}, u32[]{:S(2)}) copy-start(bf16[384,1024]{1,0:T(8,128)(2,1)} %copy-done.1) | copy-start | bytes 2359300
  1060.3 49.1 %copy-start.4 = (bf16[384,384]{1,0:T(8,128)(2,1)S(1)}, bf16[384,384]{1,0:T(8,128)(2,1)}, u32[]{:S(2)}) copy-start(bf16[384,384]{1,0:T(8,128)(2,1)} %copy-done.3) | copy-start | bytes 884740
  1060.4 18.6 %collective-permute-start.26 = (bf16[8,1024]{1,0:T(8,128)(2,1)S(1)}, bf16[8,1024]{1,0:T(8,128)(2,1)S(1)}, u32[]{:S(2)}, u32[]{:S(2)}) collective-permute-start(bf16[8,1024]{1,0:T(8,128)(2,1)S(1)} %convert.70), channel_id=1, source_target_pairs={{0,67},{1,68},{2,69},{3,70},{4,71},{5,128},{6,129},{7,130},{64,131... | collective-permute-start | bytes 49160
  1063.2 17.7 %collective-permute-start.27 = (bf16[8,1024]{1,0:T(8,128)(2,1)S(1)}, bf16[8,1024]{1,0:T(8,128)(2,1)S(1)}, u32[]{:S(2)}, u32[]{:S(2)}) collective-permute-start(bf16[8,1024]{1,0:T(8,128)(2,1)S(1)} %convert.70), channel_id=1, source_target_pairs={{0,68},{1,69},{2,70},{3,71},{4,128},{5,129},{6,130},{7,131},{64,13... | collective-permute-start | bytes 49160
  1070.2 12.6 %collective-permute-start.28 = (bf16[8,1024]{1,0:T(8,128)(2,1)S(1)}, bf16[8,1024]{1,0:T(8,128)(2,1)S(1)}, u32[]{:S(2)}, u32[]{:S(2)}) collective-permute-start(bf16[8,1024]{1,0:T(8,128)(2,1)S(1)} %convert.70), channel_id=1, source_target_pairs={{0,69},{1,70},{2,71},{3,128},{4,129},{5,130},{6,131},{7,132},{64,1... | collective-permute-start | bytes 49160
  1072.1 13.1 %collective-permute-start.29 = (bf16[8,1024]{1,0:T(8,128)(2,1)S(1)}, bf16[8,1024]{1,0:T(8,128)(2,1)S(1)}, u32[]{:S(2)}, u32[]{:S(2)}) collective-permute-start(bf16[8,1024]{1,0:T(8,128)(2,1)S(1)} %convert.70), channel_id=1, source_target_pairs={{0,70},{1,71},{2,128},{3,129},{4,130},{5,131},{6,132},{7,133},{64,... | collective-permute-start | bytes 49160
  1074.1 14.2 %collective-permute-start.30 = (bf16[8,1024]{1,0:T(8,128)(2,1)S(1)}, bf16[8,1024]{1,0:T(8,128)(2,1)S(1)}, u32[]{:S(2)}, u32[]{:S(2)}) collective-permute-start(bf16[8,1024]{1,0:T(8,128)(2,1)S(1)} %convert.70), channel_id=1, source_target_pairs={{0,71},{1,128},{2,129},{3,130},{4,131},{5,132},{6,133},{7,134},{64... | collective-permute-start | bytes 49160
  1078.9 17.6 %collective-permute-start = (bf16[8,1024]{1,0:T(8,128)(2,1)}, bf16[8,1024]{1,0:T(8,128)(2,1)S(1)}, u32[]{:S(2)}, u32[]{:S(2)}) collective-permute-start(bf16[8,1024]{1,0:T(8,128)(2,1)} %convert.71), channel_id=1, source_target_pairs={{0,1},{1,2},{2,3},{3,4},{4,5},{5,6},{6,7},{7,64},{64,65},{65,66},{... | collective-permute-start | bytes 49160
  1080.9 17.0 %collective-permute-start.1 = (bf16[8,1024]{1,0:T(8,128)(2,1)}, bf16[8,1024]{1,0:T(8,128)(2,1)S(1)}, u32[]{:S(2)}, u32[]{:S(2)}) collective-permute-start(bf16[8,1024]{1,0:T(8,128)(2,1)} %convert.71), channel_id=1, source_target_pairs={{0,2},{1,3},{2,4},{3,5},{4,6},{5,7},{6,64},{7,65},{64,66},{65,67},... | collective-permute-start | bytes 49160
  1082.8 17.1 %collective-permute-start.10 = (bf16[8,1024]{1,0:T(8,128)(2,1)}, bf16[8,1024]{1,0:T(8,128)(2,1)S(1)}, u32[]{:S(2)}, u32[]{:S(2)}) collective-permute-start(bf16[8,1024]{1,0:T(8,128)(2,1)} %convert.71), channel_id=1, source_target_pairs={{0,67},{1,68},{2,69},{3,70},{4,71},{5,128},{6,129},{7,130},{64,131... | collective-permute-start | bytes 49160
  1085.2 16.7 %collective-permute-start.11 = (bf16[8,1024]{1,0:T(8,128)(2,1)}, bf16[8,1024]{1,0:T(8,128)(2,1)S(1)}, u32[]{:S(2)}, u32[]{:S(2)}) collective-permute-start(bf16[8,1024]{1,0:T(8,128)(2,1)} %convert.71), channel_id=1, source_target_pairs={{0,68},{1,69},{2,70},{3,71},{4,128},{5,129},{6,130},{7,131},{64,13... | collective-permute-start | bytes 49160
  1088.9 16.7 %collective-permute-start.12 = (bf16[8,1024]{1,0:T(8,128)(2,1)}, bf16[8,1024]{1,0:T(8,128)(2,1)S(1)}, u32[]{:S(2)}, u32[]{:S(2)}) collective-permute-start(bf16[8,1024]{1,0:T(8,128)(2,1)} %convert.71), channel_id=1, source_target_pairs={{0,69},{1,70},{2,71},{3,128},{4,129},{5,130},{6,131},{7,132},{64,1... | collective-permute-start | bytes 49160
  1096.6 18.8 %collective-permute-start.13 = (bf16[8,1024]{1,0:T(8,128)(2,1)}, bf16[8,1024]{1,0:T(8,128)(2,1)S(1)}, u32[]{:S(2)}, u32[]{:S(2)}) collective-permute-start(bf16[8,1024]{1,0:T(8,128)(2,1)} %convert.71), channel_id=1, source_target_pairs={{0,70},{1,71},{2,128},{3,129},{4,130},{5,131},{6,132},{7,133},{64,... | collective-permute-start | bytes 49160
  1097.9 22.0 %collective-permute-start.14 = (bf16[8,1024]{1,0:T(8,128)(2,1)}, bf16[8,1024]{1,0:T(8,128)(2,1)S(1)}, u32[]{:S(2)}, u32[]{:S(2)}) collective-permute-start(bf16[8,1024]{1,0:T(8,128)(2,1)} %convert.71), channel_id=1, source_target_pairs={{0,71},{1,128},{2,129},{3,130},{4,131},{5,132},{6,133},{7,134},{64... | collective-permute-start | bytes 49160
  1099.9 22.2 %collective-permute-start.2 = (bf16[8,1024]{1,0:T(8,128)(2,1)}, bf16[8,1024]{1,0:T(8,128)(2,1)S(1)}, u32[]{:S(2)}, u32[]{:S(2)}) collective-permute-start(bf16[8,1024]{1,0:T(8,128)(2,1)} %convert.71), channel_id=1, source_target_pairs={{0,3},{1,4},{2,5},{3,6},{4,7},{5,64},{6,65},{7,66},{64,67},{65,68}... | collective-permute-start | bytes 49160
  1101.9 22.2 %collective-permute-start.3 = (bf16[8,1024]{1,0:T(8,128)(2,1)}, bf16[8,1024]{1,0:T(8,128)(2,1)S(1)}, u32[]{:S(2)}, u32[]{:S(2)}) collective-permute-start(bf16[8,1024]{1,0:T(8,128)(2,1)} %convert.71), channel_id=1, source_target_pairs={{0,4},{1,5},{2,6},{3,7},{4,64},{5,65},{6,66},{7,67},{64,68},{65,69... | collective-permute-start | bytes 49160
  1105.6 19.8 %collective-permute-start.4 = (bf16[8,1024]{1,0:T(8,128)(2,1)}, bf16[8,1024]{1,0:T(8,128)(2,1)S(1)}, u32[]{:S(2)}, u32[]{:S(2)}) collective-permute-start(bf16[8,1024]{1,0:T(8,128)(2,1)} %convert.71), channel_id=1, source_target_pairs={{0,5},{1,6},{2,7},{3,64},{4,65},{5,66},{6,67},{7,68},{64,69},{65,7... | collective-permute-start | bytes 49160
  1111.0 16.8 %copy-start.25 = (bf16[8,1024]{1,0:T(8,128)(2,1)S(1)}, bf16[8,1024]{1,0:T(8,128)(2,1)}, u32[]{:S(2)}) copy-start(bf16[8,1024]{1,0:T(8,128)(2,1)} %copy-done.24) | copy-start | bytes 49156
  1111.0 16.8 %copy-start.29 = (bf16[8,1024]{1,0:T(8,128)(2,1)S(1)}, bf16[8,1024]{1,0:T(8,128)(2,1)}, u32[]{:S(2)}) copy-start(bf16[8,1024]{1,0:T(8,128)(2,1)} %copy-done.28) | copy-start | bytes 49156
  1115.4 11.9 %collective-permute-start.5 = (bf16[8,1024]{1,0:T(8,128)(2,1)}, bf16[8,1024]{1,0:T(8,128)(2,1)S(1)}, u32[]{:S(2)}, u32[]{:S(2)}) collective-permute-start(bf16[8,1024]{1,0:T(8,128)(2,1)} %convert.71), channel_id=1, source_target_pairs={{0,6},{1,7},{2,64},{3,65},{4,66},{5,67},{6,68},{7,69},{64,70},{65,... | collective-permute-start | bytes 49160
  1120.0 7.4 collective-permute-start.6
  1122.2 5.2 collective-permute-start.7
  1124.1 3.2 collective-permute-start.8
  1125.4 2.4 collective-permute-start.9
  (34 other events, 186.6 us)
Sparse Core Ops, SparseCore 0:
  213.1 135.1 reduce-scatter.10
  434.4 130.2 reduce-scatter.12
where the time goes:
time: 1150 us; the launch traced here: 1140 us
  blocking collectives  847 us (74%)
  waiting for transfers between devices  130 us (11%)
  starting transfers between devices  119 us (10%)
  between operations  15.9 us (1%)
  local copies, waits for them, and re-layouts  12.4 us (1%)
    unnamed x1, blocking collectives  244 us
    all_gather x1, blocking collectives, body(): lax.all_gather(output_cotangent, ('dp', 'col'), axis=0, tiled=True)  218 us
    all_gather x1, blocking collectives, body(): lax.all_gather(activations, ('dp', 'col'), axis=0, tiled=True)  203 us
    reduce_scatter x1, waiting for transfers between devices, body(): lax.psum_scatter(contract_rows(all_cotangent, down_weight).astype(jnp.bfl...  130 us
    unnamed x32, starting transfers between devices  118 us
    all_gather x1, blocking collectives, body(): lax.all_gather(gated_hidden(gate_sum, up_sum), 'row', axis=0, tiled=True)  65.2 us
    all_gather x1, blocking collectives, body(): lax.all_gather(up_slope, 'row', axis=0, tiled=True)  58.9 us
    all_gather x1, blocking collectives, body(): lax.all_gather(gate_slope, 'row', axis=0, tiled=True)  58.5 us
  transfers between devices with their start and end apart: 34, of which 2 were waited for; matrix products, arithmetic and copies ran while one was open for 1% of the time, Pallas kernels for 0%

commit v1 on v0

v1 whole, which is shorter than its diff:
```python
import jax
import jax.numpy as jnp
from jax import lax
from jax.experimental import pallas as pl
from jax.experimental.pallas import tpu as pltpu
from jax.sharding import PartitionSpec as P

MESH = pl.DeviceIdType.MESH
F32 = jnp.float32
BF16 = jnp.bfloat16
LANES = 128
OWN = 6
NX, NY, NZ = 4, 4, 8
BLOCK = OWN * NZ
HALF = NX * BLOCK
WIDTH = 1024
HID = 384
CHUNKS = WIDTH // LANES


def dot(left, right, dims):
    return lax.dot_general(left, right, (dims, ((), ())), preferred_element_type=F32)


def over_tokens(left, right):
    left, right = (v.reshape(2 * HALF, v.shape[-1]) for v in (left, right))
    return dot(left, right, ((0,), (0,))).astype(BF16)


def kernel(
    act_ref, cot_ref, gw_hbm, uw_hbm, dw_hbm,
    out_ref, inp_ref, gg_hbm, ug_hbm, dg_hbm,
    wgu, wd, zpiece, xall,
    gpart, grecv, gsend, gz, spart, srecv, ssend, sz, sums,
    hid, slope, part, crecv, xsend, xrecv, zsend, zrecv, gradg, gradu, gradd,
    wsem, osem,
    z_s, z_r, x_s, x_r, c_s, c_r, yg_s, yg_r, ys_s, ys_r, e_s, e_r,
    yh_s, yh_r, yl_s, yl_r, fc_s, fc_r, fx_s, fx_r, fz_s, fz_r,
):
    dp, row, zl = lax.axis_index("dp"), lax.axis_index("row"), lax.axis_index("col")
    x, c = dp // 2, lax.rem(dp, 2)
    y, zh = row // 2, lax.rem(row, 2)

    sib = {"dp": x * 2 + 1 - c}
    far = {"row": y * 2 + 1 - zh}

    def xpos(i):
        return lax.rem(x + i, NX)

    def ypos(i):
        return lax.rem(y + i, NY)

    def zpos(i):
        return lax.rem(zl + i, NZ)

    def xdev(i):
        return {"dp": xpos(i) * 2 + c}

    def ydev(i):
        return {"row": ypos(i) * 2 + zh}

    def zdev(i):
        return {"col": zpos(i)}

    loads = [
        pltpu.make_async_copy(gw_hbm, wgu.at[:, 0:HID], wsem.at[0]),
        pltpu.make_async_copy(uw_hbm, wgu.at[:, HID : 2 * HID], wsem.at[1]),
        pltpu.make_async_copy(dw_hbm, wd, wsem.at[2]),
    ]
    for load in loads:
        load.start()

    barrier = pltpu.get_barrier_semaphore()
    peers = [sib, far]
    peers += [xdev(i) for i in range(1, NX)]
    peers += [ydev(i) for i in range(1, NY)]
    peers += [zdev(i) for i in range(1, NZ)]
    for peer in peers:
        pl.semaphore_signal(barrier, inc=1, device_id=peer, device_id_type=MESH)

    def to_fine(value):
        return value.reshape(value.shape[0] * CHUNKS, LANES)

    def from_fine(value):
        return value.reshape(value.shape[0] // CHUNKS, WIDTH)

    for kind, ref in ((0, act_ref), (1, cot_ref)):
        zpiece[kind, zl] = to_fine(ref[...].astype(F32)).astype(BF16)

    pl.semaphore_wait(barrier, len(peers))

    started = []

    def send(src, dst, s, r, device):
        copy = pltpu.make_async_remote_copy(
            src_ref=src, dst_ref=dst, send_sem=s, recv_sem=r, device_id=device, device_id_type=MESH
        )
        copy.start()
        started.append(copy)
        return copy

    def z_gather(kind):
        return [
            send(zpiece.at[kind, zl], zpiece.at[kind, zl], z_s.at[kind, i], z_r.at[kind, i], zdev(i + 1))
            for i in range(NZ - 1)
        ]

    def forward(kind, where, i):
        block = xall.at[kind, c, where]
        return send(block, block, c_s.at[kind, i], c_r.at[kind, i], sib)

    def x_gather(kind, copies):
        for copy in copies:
            copy.wait_recv()
        pieces = zpiece[kind].reshape(NZ * OWN * CHUNKS, LANES).astype(F32)
        xall[kind, c, x] = from_fine(pieces).astype(BF16)
        block = xall.at[kind, c, x]
        xs = [
            send(block, block, x_s.at[kind, i], x_r.at[kind, i], xdev(i + 1))
            for i in range(NX - 1)
        ]
        return xs, [forward(kind, x, 0)]

    def pass_on(kind, xs, cs):
        for i in (0, 2, 1):
            xs[i].wait_recv()
            cs.append(forward(kind, lax.rem(x + NX - i - 1, NX), i + 1))

    def y_scatter(t, parts, recv, s, r):
        return [
            send(parts.at[t, ypos(i + 1)], recv.at[t, i], s.at[t, i], r.at[t, i], ydev(i + 1))
            for i in range(NY - 1)
        ]

    def y_gather(t, buf, s, r):
        return [
            send(buf.at[t, y], buf.at[t, y], s.at[t, i], r.at[t, i], ydev(i + 1))
            for i in range(NY - 1)
        ]

    def y_sum(t, copies, parts, recv, out):
        total = parts[t, y].astype(F32)
        for i in (0, 2, 1):
            copies[i].wait_recv()
            total = total + recv[t, i].astype(F32)
        out[t] = total.astype(BF16)

    def received(copies):
        for copy in copies:
            copy.wait_recv()

    az = z_gather(0)
    ax, ac = x_gather(0, az)
    cz = z_gather(1)
    pass_on(0, ax, ac)
    loads[0].wait()
    loads[1].wait()
    received(ac)

    yg = []
    for t in range(2):
        gpart[t] = (
            dot(xall[0, t].reshape(HALF, WIDTH), wgu[...], ((1,), (0,)))
            .astype(BF16)
            .reshape(NY, BLOCK, 2 * HID)
        )
        yg.append(y_scatter(t, gpart, grecv, yg_s, yg_r))

    eg = []

    def exchange(t, k, src, dst):
        return send(src.at[t], dst.at[t], e_s.at[k, t], e_r.at[k, t], far)

    cx, cc = x_gather(1, cz)
    y_sum(0, yg[0], gpart, grecv, gsend)
    eg.append(exchange(0, 0, gsend, gz))
    pass_on(1, cx, cc)
    y_sum(1, yg[1], gpart, grecv, gsend)
    eg.append(exchange(1, 0, gsend, gz))
    loads[2].wait()
    received(cc)

    ys, es = [], []
    for t in range(2):
        spart[t] = (
            dot(xall[1, t].reshape(HALF, WIDTH), wd[...], ((1,), (1,)))
            .astype(BF16)
            .reshape(NY, BLOCK, HID)
        )
        ys.append(y_scatter(t, spart, srecv, ys_s, ys_r))
    for t in range(2):
        y_sum(t, ys[t], spart, srecv, ssend)
        es.append(exchange(t, 1, ssend, sz))

    yh = []
    for t in range(2):
        eg[t].wait_recv()
        both = gsend[t].astype(F32) + gz[t].astype(F32)
        sums[t] = both
        gate, up = both[:, 0:HID], both[:, HID : 2 * HID]
        hid[t, y] = (gate * jax.nn.sigmoid(gate) * up).astype(BF16)
        yh.append(y_gather(t, hid, yh_s, yh_r))

    def scatter_core(k, t):
        return pltpu.make_async_remote_copy(
            src_ref=part.at[k, t], dst_ref=crecv.at[k], send_sem=fc_s.at[k],
            recv_sem=fc_r.at[k], device_id=sib, device_id_type=MESH,
        )

    def scatter_x(k):
        scatter_core(k, 1 - c).wait_recv()
        xsend[k] = (part[k, c].astype(F32) + crecv[k].astype(F32)).astype(BF16)
        return [
            send(xsend.at[k, xpos(i + 1)], xrecv.at[k, i], fx_s.at[k, i], fx_r.at[k, i], xdev(i + 1))
            for i in range(NX - 1)
        ]

    def scatter_z(k, copies):
        total = xsend[k, x].astype(F32)
        for i in (0, 2, 1):
            copies[i].wait_recv()
            total = total + xrecv[k, i].astype(F32)
        zsend[k] = to_fine(total).astype(BF16).reshape(NZ, OWN * CHUNKS, LANES)
        return [
            send(zsend.at[k, zpos(i + 1)], zrecv.at[k, i], fz_s.at[k, i], fz_r.at[k, i], zdev(i + 1))
            for i in range(NZ - 1)
        ]

    def finish(k, copies, ref):
        total = zsend[k, zl].astype(F32)
        for i in range(NZ - 1):
            copies[i].wait_recv()
            total = total + zrecv[k, i].astype(F32)
        ref[...] = from_fine(total).astype(BF16)

    for t in range(2):
        received(yh[t])
        part[0, t] = (
            dot(hid[t].reshape(HALF, HID), wd[...], ((1,), (0,))).astype(BF16).reshape(NX, BLOCK, WIDTH)
        )
    scatter_core(0, 1 - c).start()
    fx_o = scatter_x(0)
    cots = xall.at[1]

    @pl.loop(0, HID // LANES)
    def _(j):
        at = pl.ds(pl.multiple_of(j * LANES, LANES), LANES)
        gradd[at, :] = over_tokens(hid[:, :, :, at], cots[...])

    stores = [pltpu.make_async_copy(gradd, dg_hbm, osem.at[0])]
    stores[0].start()

    yl = []
    for t in range(2):
        es[t].wait_recv()
        both = sums[t]
        gate, up = both[:, 0:HID], both[:, HID : 2 * HID]
        ds = ssend[t].astype(F32) + sz[t].astype(F32)
        s = jax.nn.sigmoid(gate)
        slope[t, y, :, 0:HID] = (ds * up * s * (1.0 + gate * (1.0 - s))).astype(BF16)
        slope[t, y, :, HID : 2 * HID] = (ds * gate * s).astype(BF16)
        yl.append(y_gather(t, slope, yl_s, yl_r))
        if t == 0:
            fz_o = scatter_z(0, fx_o)

    for t in range(2):
        received(yl[t])
        part[1, t] = (
            dot(slope[t].reshape(HALF, 2 * HID), wgu[...], ((1,), (1,)))
            .astype(BF16)
            .reshape(NX, BLOCK, WIDTH)
        )

        @pl.when(c == 1 - t)
        def _():
            scatter_core(1, t).start()

        if t == 0:
            finish(0, fz_o, out_ref)

    fx_i = scatter_x(1)

    @pl.loop(0, CHUNKS)
    def _(j):
        at = pl.ds(pl.multiple_of(j * LANES, LANES), LANES)
        gradg[at, :] = over_tokens(xall[0, :, :, :, at], slope[:, :, :, 0:HID])

    stores.append(pltpu.make_async_copy(gradg, gg_hbm, osem.at[1]))
    stores[1].start()
    fz_i = scatter_z(1, fx_i)

    @pl.loop(0, CHUNKS)
    def _(j):
        at = pl.ds(pl.multiple_of(j * LANES, LANES), LANES)
        gradu[at, :] = over_tokens(xall[0, :, :, :, at], slope[:, :, :, HID : 2 * HID])

    stores.append(pltpu.make_async_copy(gradu, ug_hbm, osem.at[2]))
    stores[2].start()
    finish(1, fz_i, inp_ref)
    for k in range(2):
        scatter_core(k, 1 - c).wait_send()
    for copy in started:
        copy.wait_send()
    for store in stores:
        store.wait()


def body(activations, gate_weight, up_weight, down_weight, output_cotangent):
    vmem = pl.BlockSpec(memory_space=pltpu.VMEM)
    hbm = pl.BlockSpec(memory_space=pl.ANY)
    dma = pltpu.SemaphoreType.DMA
    small = jax.ShapeDtypeStruct((OWN, WIDTH), BF16)
    tall = jax.ShapeDtypeStruct((WIDTH, HID), BF16)
    scratch = [
        pltpu.VMEM((WIDTH, 2 * HID), BF16),
        pltpu.VMEM((HID, WIDTH), BF16),
        pltpu.VMEM((2, NZ, OWN * CHUNKS, LANES), BF16),
        pltpu.VMEM((2, 2, NX, BLOCK, WIDTH), BF16),
        pltpu.VMEM((2, NY, BLOCK, 2 * HID), BF16),
        pltpu.VMEM((2, NY - 1, BLOCK, 2 * HID), BF16),
        pltpu.VMEM((2, BLOCK, 2 * HID), BF16),
        pltpu.VMEM((2, BLOCK, 2 * HID), BF16),
        pltpu.VMEM((2, NY, BLOCK, HID), BF16),
        pltpu.VMEM((2, NY - 1, BLOCK, HID), BF16),
        pltpu.VMEM((2, BLOCK, HID), BF16),
        pltpu.VMEM((2, BLOCK, HID), BF16),
        pltpu.VMEM((2, BLOCK, 2 * HID), F32),
        pltpu.VMEM((2, NY, BLOCK, HID), BF16),
        pltpu.VMEM((2, NY, BLOCK, 2 * HID), BF16),
        pltpu.VMEM((2, 2, NX, BLOCK, WIDTH), BF16),
        pltpu.VMEM((2, NX, BLOCK, WIDTH), BF16),
        pltpu.VMEM((2, NX, BLOCK, WIDTH), BF16),
        pltpu.VMEM((2, NX - 1, BLOCK, WIDTH), BF16),
        pltpu.VMEM((2, NZ, OWN * CHUNKS, LANES), BF16),
        pltpu.VMEM((2, NZ - 1, OWN * CHUNKS, LANES), BF16),
        pltpu.VMEM((WIDTH, HID), BF16),
        pltpu.VMEM((WIDTH, HID), BF16),
        pltpu.VMEM((HID, WIDTH), BF16),
        dma((3,)),
        dma((3,)),
    ]
    for shape in (
        (2, NZ - 1), (2, NX - 1), (2, NX), (2, NY - 1), (2, NY - 1), (2, 2),
        (2, NY - 1), (2, NY - 1), (2,), (2, NX - 1), (2, NZ - 1),
    ):
        scratch += [dma(shape), dma(shape)]
    return pl.pallas_call(
        kernel,
        out_shape=(small, small, tall, tall, jax.ShapeDtypeStruct((HID, WIDTH), BF16)),
        in_specs=[vmem, vmem, hbm, hbm, hbm],
        out_specs=(vmem, vmem, hbm, hbm, hbm),
        scratch_shapes=scratch,
        compiler_params=pltpu.CompilerParams(
            collective_id=0, has_side_effects=True, vmem_limit_bytes=44 << 20
        ),
    )(activations, output_cotangent, gate_weight, up_weight, down_weight)


def solution(mesh):
    in_specs = (
        P(("dp", "col"), "row"),
        P("row", ("dp", "col")),
        P("row", ("dp", "col")),
        P(("dp", "col"), "row"),
        P(("dp", "col"), "row"),
    )
    out_specs = (
        P(("dp", "col"), "row"),
        P(("dp", "col"), "row"),
        P("row", ("dp", "col")),
        P("row", ("dp", "col")),
        P(("dp", "col"), "row"),
    )
    return jax.shard_map(body, mesh=mesh, in_specs=in_specs, out_specs=out_specs, check_vma=False)
```

time: 1150 us -> 102 us (0.09); the launches traced: 1140 us -> 101 us
  blocking collectives: 847 us -> 0 us
  waiting for transfers between devices: 130 us -> 0 us
  starting transfers between devices: 119 us -> 0 us
  Pallas kernels: 0 us -> 91.9 us
  between operations: 15.9 us -> 0.66 us
    all_gather x5 -> x0, blocking collectives: 604 us -> none  [the longest x1 218 us: body(): lax.all_gather(output_cotangent, ('dp', 'col'), axis=0, tiled=True)]
    unnamed x1 -> x0, blocking collectives: 244 us -> none
    reduce_scatter x2 -> x0, waiting for transfers between devices: 130 us -> none  [the longest x1 130 us: body(): lax.psum_scatter(contract_rows(all_cotangent, down_weight).astype(jnp.bfl...]
    unnamed x32 -> x0, starting transfers between devices: 118 us -> none
    pallas_call x0 -> x1, Pallas kernels: none -> 91.9 us  [body(): pl.pallas_call(kernel, out_shape=(small, small, tall, tall, jax.ShapeDtyp...]
  transfers between devices with their start and end apart: 34 -> 0, of which waited for: 2 -> 0; matrix products, arithmetic and copies ran while one was open for 1% -> 0% of each run, Pallas kernels for 0% -> 0%
where the time goes in v1:
time: 102 us; the launch traced here: 101 us
  Pallas kernels  91.9 us (90%)
  local copies, waits for them, and re-layouts  8.67 us (8%)
    pallas_call x1, Pallas kernels, body(): pl.pallas_call(kernel, out_shape=(small, small, tall, tall, jax.ShapeDtyp...  91.9 us
    unnamed x15, local copies, waits for them, and re-layouts  8.67 us

profile of v1, /device:TPU:1, one launch (start us, length us, event | category | flops | bytes accessed | tf_op | source)
XLA Modules:
  0.0 101.2 jit_solution(34298944588724082)
XLA Ops:
  0.6 0.0 copy-start
  0.6 1.1 %copy-done = bf16[1024,384]{1,0:T(8,128)(2,1)S(1)} copy-done((bf16[1024,384]{1,0:T(8,128)(2,1)S(1)}, bf16[1024,384]{1,0:T(8,128)(2,1)}, u32[]{:S(2)}) %copy-start) | copy-done | bytes 786456
  1.8 0.0 copy-start.1
  1.8 1.1 %copy-done.1 = bf16[1024,384]{1,0:T(8,128)(2,1)S(1)} copy-done((bf16[1024,384]{1,0:T(8,128)(2,1)S(1)}, bf16[1024,384]{1,0:T(8,128)(2,1)}, u32[]{:S(2)}) %copy-start.1) | copy-done | bytes 786456
  2.9 0.0 copy-start.2
  2.9 1.1 %copy-done.2 = bf16[384,1024]{1,0:T(8,128)(2,1)S(1)} copy-done((bf16[384,1024]{1,0:T(8,128)(2,1)S(1)}, bf16[384,1024]{1,0:T(8,128)(2,1)}, u32[]{:S(2)}) %copy-start.2) | copy-done | bytes 786456
  4.0 0.0 copy-start.3
  4.0 0.7 copy-done.3
  4.8 0.0 copy-start.4
  4.8 0.7 copy-done.4
  5.5 91.9 %shard_map.92 = (bf16[6,1024]{1,0:T(8,128)(2,1)S(1)}, bf16[6,1024]{1,0:T(8,128)(2,1)S(1)}, bf16[1024,384]{1,0:T(8,128)(2,1)S(1)}, bf16[1024,384]{1,0:T(8,128)(2,1)S(1)}, bf16[384,1024]{1,0:T(8,128)(2,1)S(1)}) custom-call(bf16[6,1024]{1,0:T(8,128)(2,1)S(1)} %copy-done.3, bf16[6,1024]{1,0:T(8,128)(2,1)S(1)} %copy-done.4, bf16[1024,384]{1,0:T(8,128)(2,1)S(1)} %copy-done, ...), custom_call_target="tpu_custom_call" | custom-call | tf_op jit(solution)/shard_map/pallas_call | solution.py:347
  97.3 0.6 copy.15
  98.0 0.6 copy.16
  98.6 0.9 copy.17
  99.4 0.9 copy.18
  100.3 0.9 copy.19
Async XLA Ops:
  0.6 1.1 %copy-start = (bf16[1024,384]{1,0:T(8,128)(2,1)S(1)}, bf16[1024,384]{1,0:T(8,128)(2,1)}, u32[]{:S(2)}) copy-start(bf16[1024,384]{1,0:T(8,128)(2,1)} %gw_hbm.1) | copy-start | bytes 2359300
  1.8 1.1 %copy-start.1 = (bf16[1024,384]{1,0:T(8,128)(2,1)S(1)}, bf16[1024,384]{1,0:T(8,128)(2,1)}, u32[]{:S(2)}) copy-start(bf16[1024,384]{1,0:T(8,128)(2,1)} %uw_hbm.1) | copy-start | bytes 2359300
  2.9 1.1 %copy-start.2 = (bf16[384,1024]{1,0:T(8,128)(2,1)S(1)}, bf16[384,1024]{1,0:T(8,128)(2,1)}, u32[]{:S(2)}) copy-start(bf16[384,1024]{1,0:T(8,128)(2,1)} %dw_hbm.1) | copy-start | bytes 2359300
  4.0 0.7 copy-start.3
  4.8 0.7 copy-start.4

commit v2 on v1

v2 whole, which is shorter than its diff:
```python
import jax
import jax.numpy as jnp
from jax import lax
from jax.experimental import pallas as pl
from jax.experimental.pallas import tpu as pltpu
from jax.sharding import PartitionSpec as P

MESH = pl.DeviceIdType.MESH
F32 = jnp.float32
BF16 = jnp.bfloat16
LANES = 128
OWN = 6
NX, NY, NZ = 4, 4, 8
BLOCK = OWN * NZ
HALF = NX * BLOCK
WIDTH = 1024
HID = 384
CHUNKS = WIDTH // LANES


def dot(left, right, dims):
    return lax.dot_general(left, right, (dims, ((), ())), preferred_element_type=F32)


def over_tokens(left, right):
    left, right = (v.reshape(2 * HALF, v.shape[-1]) for v in (left, right))
    return dot(left, right, ((0,), (0,))).astype(BF16)


def kernel(
    act_hbm, cot_hbm, gw_hbm, uw_hbm, dw_hbm,
    out_hbm, inp_hbm, gg_hbm, ug_hbm, dg_hbm,
    mine, wgu, wd, acts_t, zpiece, xall,
    gpart, grecv, gsend, gz, spart, srecv, ssend, sz, sums,
    hid, slope, part, crecv, xsend, xrecv, zsend, zrecv, rows_out, gradg, gradu, gradd, wsem, osem,
    z_s, z_r, x_s, x_r, c_s, c_r, yg_s, yg_r, ys_s, ys_r, e_s, e_r,
    yh_s, yh_r, yl_s, yl_r, fc_s, fc_r, fx_s, fx_r, fz_s, fz_r,
):
    dp, row, zl = lax.axis_index("dp"), lax.axis_index("row"), lax.axis_index("col")
    x, c = dp // 2, lax.rem(dp, 2)
    y, zh = row // 2, lax.rem(row, 2)

    sib = {"dp": x * 2 + 1 - c}
    far = {"row": y * 2 + 1 - zh}

    def xpos(i):
        return lax.rem(x + i, NX)

    def ypos(i):
        return lax.rem(y + i, NY)

    def zpos(i):
        return lax.rem(zl + i, NZ)

    def xdev(i):
        return {"dp": xpos(i) * 2 + c}

    def ydev(i):
        return {"row": ypos(i) * 2 + zh}

    def zdev(i):
        return {"col": zpos(i)}

    loads = [
        pltpu.make_async_copy(act_hbm, mine.at[0], wsem.at[3]),
        pltpu.make_async_copy(cot_hbm, mine.at[1], wsem.at[4]),
        pltpu.make_async_copy(gw_hbm, wgu.at[:, 0:HID], wsem.at[0]),
        pltpu.make_async_copy(uw_hbm, wgu.at[:, HID : 2 * HID], wsem.at[1]),
        pltpu.make_async_copy(dw_hbm, wd, wsem.at[2]),
    ]
    for load in loads:
        load.start()

    barrier = pltpu.get_barrier_semaphore()
    peers = [sib, far]
    peers += [xdev(i) for i in range(1, NX)]
    peers += [ydev(i) for i in range(1, NY)]
    peers += [zdev(i) for i in range(1, NZ)]
    for peer in peers:
        pl.semaphore_signal(barrier, inc=1, device_id=peer, device_id_type=MESH)

    def to_fine(value):
        return value.reshape(value.shape[0] * CHUNKS, LANES)

    def from_fine(value):
        return value.reshape(value.shape[0] // CHUNKS, WIDTH)

    for kind in range(2):
        loads[kind].wait()
        zpiece[kind, zl] = to_fine(mine[kind].astype(F32)).astype(BF16)

    pl.semaphore_wait(barrier, len(peers))

    started = []

    def send(src, dst, s, r, device):
        copy = pltpu.make_async_remote_copy(
            src_ref=src, dst_ref=dst, send_sem=s, recv_sem=r, device_id=device, device_id_type=MESH
        )
        copy.start()
        started.append(copy)
        return copy

    def z_gather(kind):
        return [
            send(zpiece.at[kind, zl], zpiece.at[kind, zl], z_s.at[kind, i], z_r.at[kind, i], zdev(i + 1))
            for i in range(NZ - 1)
        ]

    def forward(kind, where, i):
        block = xall.at[kind, c, where]
        return send(block, block, c_s.at[kind, i], c_r.at[kind, i], sib)

    def x_gather(kind, copies):
        for copy in copies:
            copy.wait_recv()
        pieces = zpiece[kind].reshape(NZ * OWN * CHUNKS, LANES).astype(F32)
        xall[kind, c, x] = from_fine(pieces).astype(BF16)
        block = xall.at[kind, c, x]
        xs = [
            send(block, block, x_s.at[kind, i], x_r.at[kind, i], xdev(i + 1))
            for i in range(NX - 1)
        ]
        return xs, [forward(kind, x, 0)]

    def pass_on(kind, xs, cs):
        for i in (0, 2, 1):
            xs[i].wait_recv()
            cs.append(forward(kind, lax.rem(x + NX - i - 1, NX), i + 1))

    def y_scatter(t, parts, recv, s, r):
        return [
            send(parts.at[t, ypos(i + 1)], recv.at[t, i], s.at[t, i], r.at[t, i], ydev(i + 1))
            for i in range(NY - 1)
        ]

    def y_gather(t, buf, s, r):
        return [
            send(buf.at[t, y], buf.at[t, y], s.at[t, i], r.at[t, i], ydev(i + 1))
            for i in range(NY - 1)
        ]

    def y_sum(t, copies, parts, recv, out):
        total = parts[t, y].astype(F32)
        for i in (0, 2, 1):
            copies[i].wait_recv()
            total = total + recv[t, i].astype(F32)
        out[t] = total.astype(BF16)

    stores = []

    def write(i, src, dst):
        stores.append(pltpu.make_async_copy(src, dst, osem.at[i]))
        stores[-1].start()

    def received(copies):
        for copy in copies:
            copy.wait_recv()

    def core_copy(k):
        return pltpu.make_async_remote_copy(
            src_ref=part.at[k, 1 - c], dst_ref=crecv.at[k], send_sem=fc_s.at[k],
            recv_sem=fc_r.at[k], device_id=sib, device_id_type=MESH,
        )

    def x_copy(k, i):
        return pltpu.make_async_remote_copy(
            src_ref=xsend.at[k, xpos(i + 1)], dst_ref=xrecv.at[k, i], send_sem=fx_s.at[k, i],
            recv_sem=fx_r.at[k, i], device_id=xdev(i + 1), device_id_type=MESH,
        )

    def scatter_core(k, t):
        @pl.when(c == 1 - t)
        def _():
            core_copy(k).start()

    def scatter_x(k, t):
        @pl.when(c == t)
        def _():
            core_copy(k).wait_recv()
            xsend[k] = (part[k, c].astype(F32) + crecv[k].astype(F32)).astype(BF16)
            for i in range(NX - 1):
                x_copy(k, i).start()

    def scatter_z(k):
        total = xsend[k, x].astype(F32)
        for i in (0, 2, 1):
            x_copy(k, i).wait_recv()
            total = total + xrecv[k, i].astype(F32)
        zsend[k] = to_fine(total).astype(BF16).reshape(NZ, OWN * CHUNKS, LANES)
        return [
            send(zsend.at[k, zpos(i + 1)], zrecv.at[k, i], fz_s.at[k, i], fz_r.at[k, i], zdev(i + 1))
            for i in range(NZ - 1)
        ]

    def finish(k, copies):
        total = zsend[k, zl].astype(F32)
        for i in range(NZ - 1):
            copies[i].wait_recv()
            total = total + zrecv[k, i].astype(F32)
        rows_out[k] = from_fine(total).astype(BF16)
        write(k, rows_out.at[k], (out_hbm, inp_hbm)[k])

    def exchange(t, k, src, dst):
        return send(src.at[t], dst.at[t], e_s.at[k, t], e_r.at[k, t], far)

    def block_terms(kind, t, weight, dims, parts):
        terms = dot(xall[kind, t].reshape(HALF, WIDTH), weight[...], dims)
        parts[t] = terms.astype(BF16).reshape(NY, BLOCK, terms.shape[-1])

    def hidden_units(t):
        both = gsend[t].astype(F32) + gz[t].astype(F32)
        sums[t] = both
        gate, up = both[:, 0:HID], both[:, HID : 2 * HID]
        hid[t, y] = (gate * jax.nn.sigmoid(gate) * up).astype(BF16)
        return y_gather(t, hid, yh_s, yh_r)

    def slope_pair(t):
        both = sums[t]
        gate, up = both[:, 0:HID], both[:, HID : 2 * HID]
        ds = ssend[t].astype(F32) + sz[t].astype(F32)
        s = jax.nn.sigmoid(gate)
        slope[t, y, :, 0:HID] = (ds * up * s * (1.0 + gate * (1.0 - s))).astype(BF16)
        slope[t, y, :, HID : 2 * HID] = (ds * gate * s).astype(BF16)
        return y_gather(t, slope, yl_s, yl_r)

    def outputs(t):
        total = dot(hid[t].reshape(HALF, HID), wd[...], ((1,), (0,)))
        part[0, t] = total.astype(BF16).reshape(NX, BLOCK, WIDTH)

    def input_slopes(t):
        total = dot(slope[t].reshape(HALF, 2 * HID), wgu[...], ((1,), (1,)))
        part[1, t] = total.astype(BF16).reshape(NX, BLOCK, WIDTH)

    az = z_gather(0)
    ax, ac = x_gather(0, az)
    cz = z_gather(1)
    pass_on(0, ax, ac)
    cx, cc = x_gather(1, cz)
    received(ac)
    loads[2].wait()
    loads[3].wait()

    yg, ys, eg, es = [], [], [], []
    for t in range(2):
        block_terms(0, t, wgu, ((1,), (0,)), gpart)
        yg.append(y_scatter(t, gpart, grecv, yg_s, yg_r))
    pass_on(1, cx, cc)
    y_sum(0, yg[0], gpart, grecv, gsend)
    eg.append(exchange(0, 0, gsend, gz))
    loads[4].wait()
    received(cc)
    for t in range(2):
        block_terms(1, t, wd, ((1,), (1,)), spart)
        ys.append(y_scatter(t, spart, srecv, ys_s, ys_r))
    y_sum(1, yg[1], gpart, grecv, gsend)
    eg.append(exchange(1, 0, gsend, gz))
    for t in range(2):
        y_sum(t, ys[t], spart, srecv, ssend)
        es.append(exchange(t, 1, ssend, sz))

    @pl.loop(0, CHUNKS)
    def _(j):
        at = pl.ds(pl.multiple_of(j * LANES, LANES), LANES)
        acts_t[at, :] = xall[0, :, :, :, at].reshape(2 * HALF, LANES).T

    received(eg[0:1])
    yh = [hidden_units(0)]
    received(yh[0])
    outputs(0)
    scatter_core(0, 0)
    received(eg[1:2])
    yh.append(hidden_units(1))
    scatter_x(0, 0)
    received(es[0:1])
    yl = [slope_pair(0)]
    received(yh[1])
    outputs(1)
    scatter_core(0, 1)
    scatter_x(0, 1)
    @pl.loop(0, HID // LANES)
    def _(j):
        at = pl.ds(pl.multiple_of(j * LANES, LANES), LANES)
        gradd[at, :] = over_tokens(hid[:, :, :, at], xall[1])

    write(4, gradd, dg_hbm)
    received(es[1:2])
    yl.append(slope_pair(1))
    received(yl[0])
    input_slopes(0)
    scatter_core(1, 0)
    fz_o = scatter_z(0)
    scatter_x(1, 0)
    received(yl[1])
    input_slopes(1)
    scatter_core(1, 1)
    scatter_x(1, 1)
    @pl.loop(0, CHUNKS // 2)
    def _(j):
        at = pl.ds(pl.multiple_of(j * 2 * LANES, 2 * LANES), 2 * LANES)
        grads = dot(acts_t[at, :], slope[...].reshape(2 * HALF, 2 * HID), ((1,), (0,)))
        gradg[at, :] = grads[:, 0:HID].astype(BF16)
        gradu[at, :] = grads[:, HID : 2 * HID].astype(BF16)

    write(2, gradg, gg_hbm)
    write(3, gradu, ug_hbm)
    finish(0, fz_o)
    fz_i = scatter_z(1)
    finish(1, fz_i)
    for k in range(2):
        core_copy(k).wait_send()
        for i in range(NX - 1):
            x_copy(k, i).wait_send()
    for copy in started:
        copy.wait_send()
    for copy in stores:
        copy.wait()


def store(*refs):
    given, results, held = refs[0:5], refs[5:10], refs[10:15]
    sems = refs[15]
    copies = []
    for i in range(5):
        copies.append(
            (
                pltpu.make_async_copy(given[i], held[i], sems.at[0, i]),
                pltpu.make_async_copy(held[i], results[i], sems.at[1, i]),
            )
        )
        copies[i][0].start()
    for read, write in copies:
        read.wait()
        write.start()
    for _, write in copies:
        write.wait()


def body(activations, gate_weight, up_weight, down_weight, output_cotangent):
    hbm = pl.BlockSpec(memory_space=pltpu.HBM)
    dma = pltpu.SemaphoreType.DMA
    small = jax.ShapeDtypeStruct((OWN, WIDTH), BF16)
    tall = jax.ShapeDtypeStruct((WIDTH, HID), BF16)
    scratch = [
        pltpu.VMEM((2, OWN, WIDTH), BF16),
        pltpu.VMEM((WIDTH, 2 * HID), BF16),
        pltpu.VMEM((HID, WIDTH), BF16),
        pltpu.VMEM((WIDTH, 2 * HALF), BF16),
        pltpu.VMEM((2, NZ, OWN * CHUNKS, LANES), BF16),
        pltpu.VMEM((2, 2, NX, BLOCK, WIDTH), BF16),
        pltpu.VMEM((2, NY, BLOCK, 2 * HID), BF16),
        pltpu.VMEM((2, NY - 1, BLOCK, 2 * HID), BF16),
        pltpu.VMEM((2, BLOCK, 2 * HID), BF16),
        pltpu.VMEM((2, BLOCK, 2 * HID), BF16),
        pltpu.VMEM((2, NY, BLOCK, HID), BF16),
        pltpu.VMEM((2, NY - 1, BLOCK, HID), BF16),
        pltpu.VMEM((2, BLOCK, HID), BF16),
        pltpu.VMEM((2, BLOCK, HID), BF16),
        pltpu.VMEM((2, BLOCK, 2 * HID), F32),
        pltpu.VMEM((2, NY, BLOCK, HID), BF16),
        pltpu.VMEM((2, NY, BLOCK, 2 * HID), BF16),
        pltpu.VMEM((2, 2, NX, BLOCK, WIDTH), BF16),
        pltpu.VMEM((2, NX, BLOCK, WIDTH), BF16),
        pltpu.VMEM((2, NX, BLOCK, WIDTH), BF16),
        pltpu.VMEM((2, NX - 1, BLOCK, WIDTH), BF16),
        pltpu.VMEM((2, NZ, OWN * CHUNKS, LANES), BF16),
        pltpu.VMEM((2, NZ - 1, OWN * CHUNKS, LANES), BF16),
        pltpu.VMEM((2, OWN, WIDTH), BF16),
        pltpu.VMEM((WIDTH, HID), BF16),
        pltpu.VMEM((WIDTH, HID), BF16),
        pltpu.VMEM((HID, WIDTH), BF16),
        dma((5,)),
        dma((5,)),
    ]
    for shape in (
        (2, NZ - 1), (2, NX - 1), (2, NX), (2, NY - 1), (2, NY - 1), (2, 2),
        (2, NY - 1), (2, NY - 1), (2,), (2, NX - 1), (2, NZ - 1),
    ):
        scratch += [dma(shape), dma(shape)]
    shapes = (small, small, tall, tall, jax.ShapeDtypeStruct((HID, WIDTH), BF16))
    results = pl.pallas_call(
        kernel,
        out_shape=shapes,
        in_specs=[hbm] * 5,
        out_specs=(hbm,) * 5,
        scratch_shapes=scratch,
        compiler_params=pltpu.CompilerParams(
            collective_id=0, has_side_effects=True, vmem_limit_bytes=61 << 20
        ),
    )(activations, output_cotangent, gate_weight, up_weight, down_weight)
    return pl.pallas_call(
        store,
        out_shape=shapes,
        in_specs=[hbm] * 5,
        out_specs=(hbm,) * 5,
        scratch_shapes=[pltpu.VMEM(s.shape, s.dtype) for s in shapes] + [dma((2, 5))],
    )(*results)


def solution(mesh):
    in_specs = (
        P(("dp", "col"), "row"),
        P("row", ("dp", "col")),
        P("row", ("dp", "col")),
        P(("dp", "col"), "row"),
        P(("dp", "col"), "row"),
    )
    out_specs = (
        P(("dp", "col"), "row"),
        P(("dp", "col"), "row"),
        P("row", ("dp", "col")),
        P("row", ("dp", "col")),
        P(("dp", "col"), "row"),
    )
    return jax.shard_map(body, mesh=mesh, in_specs=in_specs, out_specs=out_specs, check_vma=False)
```

time: 102 us -> 89.2 us (0.87)
  local copies, waits for them, and re-layouts: 8.67 us -> 0 us
  Pallas kernels: 91.9 us -> 88.2 us
    unnamed x15 -> x0, local copies, waits for them, and re-layouts: 8.67 us -> none
    pallas_call x1 -> x2, Pallas kernels: 91.9 us -> 88.2 us  [the longest x1 85.6 us: body(): pl.pallas_call(kernel, out_shape=shapes, in_specs=[hbm] * 5, out_specs=(h...]
where the time goes in v2:
time: 89.2 us; the launch traced here: 88.9 us
  Pallas kernels  88.2 us (99%)
    pallas_call x1, Pallas kernels, body(): pl.pallas_call(kernel, out_shape=shapes, in_specs=[hbm] * 5, out_specs=(h...  85.6 us
    pallas_call x1, Pallas kernels, body(): pl.pallas_call(store, out_shape=shapes, in_specs=[hbm] * 5, out_specs=(hb...  2.65 us

profile of v2, /device:TPU:1, one launch (start us, length us, event | category | flops | bytes accessed | tf_op | source)
XLA Modules:
  0.0 88.9 jit_solution(15834007412814560821)
XLA Ops:
  0.6 85.6 %shard_map.92 = (bf16[6,1024]{1,0:T(8,128)(2,1)}, bf16[6,1024]{1,0:T(8,128)(2,1)}, bf16[1024,384]{1,0:T(8,128)(2,1)}, bf16[1024,384]{1,0:T(8,128)(2,1)}, bf16[384,1024]{1,0:T(8,128)(2,1)}) custom-call(bf16[6,1024]{1,0:T(8,128)(2,1)} %act_hbm.1, bf16[6,1024]{1,0:T(8,128)(2,1)} %cot_hbm.1, bf16[1024,384]{1,0:T(8,128)(2,1)} %gw_hbm.1, ...), custom_call_target="tpu_custom_call" | custom-call | tf_op jit(solution)/shard_map/pallas_call | solution.py:381
  86.2 2.7 %shard_map.93 = (bf16[6,1024]{1,0:T(8,128)(2,1)}, bf16[6,1024]{1,0:T(8,128)(2,1)}, bf16[1024,384]{1,0:T(8,128)(2,1)}, bf16[1024,384]{1,0:T(8,128)(2,1)}, bf16[384,1024]{1,0:T(8,128)(2,1)}) custom-call(bf16[6,1024]{1,0:T(8,128)(2,1)} %get-tuple-element.10.refs_0_, bf16[6,1024]{1,0:T(8,128)(2,1)} %get-tuple-element.11.refs_1_, ...), custom_call_target="tpu_custom_call" | custom-call | tf_op jit(solution)/shard_map/pallas_call | solution.py:391

commit v3 on v2

v3 whole, which is shorter than its diff:
```python
import jax
import jax.numpy as jnp
from jax import lax
from jax.experimental import pallas as pl
from jax.experimental.pallas import tpu as pltpu
from jax.sharding import PartitionSpec as P

MESH = pl.DeviceIdType.MESH
F32 = jnp.float32
BF16 = jnp.bfloat16
LANES = 128
OWN = 6
NX, NY, NZ = 4, 4, 8
BLOCK = OWN * NZ
HALF = NX * BLOCK
WIDTH = 1024
HID = 384
CHUNKS = WIDTH // LANES


def dot(left, right, dims):
    return lax.dot_general(left, right, (dims, ((), ())), preferred_element_type=F32)


def over_tokens(left, right):
    left, right = (v.reshape(2 * HALF, v.shape[-1]) for v in (left, right))
    return dot(left, right, ((0,), (0,))).astype(BF16)


def kernel(
    act_hbm, cot_hbm, gw_hbm, uw_hbm, dw_hbm,
    out_hbm, inp_hbm, gg_hbm, ug_hbm, dg_hbm,
    mine, wgu, wd, acts_t, xfine, xall, terms, trecv, tsend, tfar, sums,
    hid, slope, part, crecv, xsend, xrecv, zsend, zrecv, rows_out, gradg, gradu, gradd, wsem, osem,
    z_s, z_r, x_s, x_r, c_s, c_r, y_s, y_r, e_s, e_r,
    yh_s, yh_r, yl_s, yl_r, fc_s, fc_r, fx_s, fx_r, fz_s, fz_r,
):
    dp, row, zl = lax.axis_index("dp"), lax.axis_index("row"), lax.axis_index("col")
    x, c = dp // 2, lax.rem(dp, 2)
    y, zh = row // 2, lax.rem(row, 2)

    sib = {"dp": x * 2 + 1 - c}
    far = {"row": y * 2 + 1 - zh}

    half = zl // 4

    def xpos(i):
        return lax.rem(x + i, NX)

    def ypos(i):
        return lax.rem(y + i, NY)

    def zpos(m):
        place = 0
        for bit in (4, 2, 1):
            mine_ = lax.rem(zl // bit, 2)
            place = place + bit * (1 - mine_ if m & bit else mine_)
        return place

    def fours(order):
        return pl.ds(4 * (half if order == 0 else 1 - half), 4)

    def xdev(i):
        return {"dp": xpos(i) * 2 + c}

    def ydev(i):
        return {"row": ypos(i) * 2 + zh}

    def zdev(m):
        return {"col": zpos(m)}

    loads = [
        pltpu.make_async_copy(act_hbm, mine.at[0], wsem.at[3]),
        pltpu.make_async_copy(cot_hbm, mine.at[1], wsem.at[4]),
        pltpu.make_async_copy(gw_hbm, wgu.at[:, 0:HID], wsem.at[0]),
        pltpu.make_async_copy(uw_hbm, wgu.at[:, HID : 2 * HID], wsem.at[1]),
        pltpu.make_async_copy(dw_hbm, wd, wsem.at[2]),
    ]
    for load in loads:
        load.start()

    barrier = pltpu.get_barrier_semaphore()
    peers = [sib, far]
    peers += [xdev(i) for i in range(1, NX)]
    peers += [ydev(i) for i in range(1, NY)]
    peers += [zdev(m) for m in range(1, NZ)]
    for peer in peers:
        pl.semaphore_signal(barrier, inc=1, device_id=peer, device_id_type=MESH)

    def to_fine(value):
        return value.reshape(value.shape[0] * CHUNKS, LANES)

    def from_fine(value):
        return value.reshape(value.shape[0] // CHUNKS, WIDTH)

    for kind in range(2):
        loads[kind].wait()
        xfine[kind, c, x, zl] = to_fine(mine[kind].astype(F32)).astype(BF16)

    pl.semaphore_wait(barrier, len(peers))

    started = []

    def send(src, dst, s, r, device):
        copy = pltpu.make_async_remote_copy(
            src_ref=src, dst_ref=dst, send_sem=s, recv_sem=r, device_id=device, device_id_type=MESH
        )
        copy.start()
        started.append(copy)
        return copy

    def z_gather(kind):
        piece = xfine.at[kind, c, x, zl]
        copies = {}
        for m in (7, 6, 5, 4, 3, 2, 1):
            copies[m] = send(piece, piece, z_s.at[kind, m - 1], z_r.at[kind, m - 1], zdev(m))
        return copies

    def forward(kind, where, order, i):
        block = xfine.at[kind, c, where, fours(order)]
        return send(block, block, c_s.at[kind, order, i], c_r.at[kind, order, i], sib)

    def x_gather(kind, copies):
        xs, cs = [], []
        for order in range(2):
            for m in ((1, 2, 3), (4, 5, 6, 7))[order]:
                copies[m].wait_recv()
            block = xfine.at[kind, c, x, fours(order)]
            for i in range(NX - 1):
                sems = x_s.at[kind, order, i], x_r.at[kind, order, i]
                xs.append(send(block, block, *sems, xdev(i + 1)))
            cs.append(forward(kind, x, order, 0))
        return xs, cs

    def pass_on(kind, xs, cs):
        for order in range(2):
            for i in (0, 2, 1):
                xs[order * (NX - 1) + i].wait_recv()
                cs.append(forward(kind, lax.rem(x + NX - i - 1, NX), order, i + 1))

    def lay_out(kind, t):
        for where in range(NX):
            pieces = xfine[kind, t, where].reshape(BLOCK * CHUNKS, LANES)
            xall[kind, t, where] = from_fine(pieces.astype(F32)).astype(BF16)

    def y_scatter(q, k):
        return [
            send(
                terms.at[q, k, ypos(i + 1)], trecv.at[q, k, i],
                y_s.at[q, k, i], y_r.at[q, k, i], ydev(i + 1),
            )
            for i in range(NY - 1)
        ]

    def y_sum(q, k, copies):
        total = terms[q, k, y].astype(F32)
        for i in (0, 2, 1):
            copies[i].wait_recv()
            total = total + trecv[q, k, i].astype(F32)
        tsend[q, k] = total.astype(BF16)
        return send(tsend.at[q, k], tfar.at[q, k], e_s.at[q, k], e_r.at[q, k], far)

    def whole(q, k):
        return tsend[q, k].astype(F32) + tfar[q, k].astype(F32)

    def y_gather(t, k, buf, s, r):
        return [
            send(buf.at[t, y], buf.at[t, y], s.at[k, i], r.at[k, i], ydev(i + 1))
            for i in range(NY - 1)
        ]

    stores = []

    def write(i, src, dst):
        stores.append(pltpu.make_async_copy(src, dst, osem.at[i]))
        stores[-1].start()

    def received(copies):
        for copy in copies:
            copy.wait_recv()

    def core_copy(k):
        return pltpu.make_async_remote_copy(
            src_ref=part.at[k, 1 - c], dst_ref=crecv.at[k], send_sem=fc_s.at[k],
            recv_sem=fc_r.at[k], device_id=sib, device_id_type=MESH,
        )

    def x_copy(k, order, i):
        at = fours(1 - order)
        return pltpu.make_async_remote_copy(
            src_ref=xsend.at[k, xpos(i + 1), at], dst_ref=xrecv.at[k, i, at],
            send_sem=fx_s.at[k, order, i], recv_sem=fx_r.at[k, order, i],
            device_id=xdev(i + 1), device_id_type=MESH,
        )

    def scatter_core(k, t):
        @pl.when(c == 1 - t)
        def _():
            core_copy(k).start()

    def scatter_x(k, t):
        @pl.when(c == t)
        def _():
            core_copy(k).wait_recv()
            for where in range(NX):
                total = part[k, c, where].astype(F32) + crecv[k, where].astype(F32)
                xsend[k, where] = to_fine(total).astype(BF16).reshape(NZ, OWN * CHUNKS, LANES)
            for order in range(2):
                for i in range(NX - 1):
                    x_copy(k, order, i).start()

    def scatter_z(k):
        copies = []
        for order in range(2):
            at = fours(1 - order)
            total = xsend[k, x, at].astype(F32)
            for i in (0, 2, 1):
                x_copy(k, order, i).wait_recv()
                total = total + xrecv[k, i, at].astype(F32)
            zsend[k, at] = total.astype(BF16)
            for m in ((7, 6, 5, 4), (3, 2, 1))[order]:
                sems = fz_s.at[k, m - 1], fz_r.at[k, m - 1]
                copies.append(send(zsend.at[k, zpos(m)], zrecv.at[k, m - 1], *sems, zdev(m)))
        return copies

    def finish(k, copies):
        total = zsend[k, zl].astype(F32)
        received(copies)
        for i in range(NZ - 1):
            total = total + zrecv[k, i].astype(F32)
        rows_out[k] = from_fine(total).astype(BF16)
        write(k, rows_out.at[k], (out_hbm, inp_hbm)[k])

    def gate_up_terms(t, k):
        both = dot(xall[0, t].reshape(HALF, WIDTH), wgu[...], ((1,), (0,))).astype(BF16)
        copies = []
        for q in range(2):
            terms[q, k] = both[:, q * HID : (q + 1) * HID].reshape(NY, BLOCK, HID)
            copies.append(y_scatter(q, k))
        return copies

    def slope_terms(t):
        terms[2, t] = (
            dot(xall[1, t].reshape(HALF, WIDTH), wd[...], ((1,), (1,)))
            .astype(BF16)
            .reshape(NY, BLOCK, HID)
        )
        return y_scatter(2, t)

    def hidden_units(t, k):
        gate, up = whole(0, k), whole(1, k)
        sums[0, t], sums[1, t] = gate, up
        hid[t, y] = (gate * jax.nn.sigmoid(gate) * up).astype(BF16)
        return y_gather(t, k, hid, yh_s, yh_r)

    def slope_pair(t):
        gate, up, ds = sums[0, t], sums[1, t], whole(2, t)
        s = jax.nn.sigmoid(gate)
        slope[t, y, :, 0:HID] = (ds * up * s * (1.0 + gate * (1.0 - s))).astype(BF16)
        slope[t, y, :, HID : 2 * HID] = (ds * gate * s).astype(BF16)
        return y_gather(t, t, slope, yl_s, yl_r)

    def outputs(t):
        total = dot(hid[t].reshape(HALF, HID), wd[...], ((1,), (0,)))
        part[0, t] = total.astype(BF16).reshape(NX, BLOCK, WIDTH)

    def input_slopes(t):
        total = dot(slope[t].reshape(HALF, 2 * HID), wgu[...], ((1,), (1,)))
        part[1, t] = total.astype(BF16).reshape(NX, BLOCK, WIDTH)

    az = z_gather(0)
    ax, ac = x_gather(0, az)
    cz = z_gather(1)
    pass_on(0, ax, ac)
    lay_out(0, c)
    loads[2].wait()
    loads[3].wait()
    yg = [gate_up_terms(c, 0)]
    received(ac)
    lay_out(0, 1 - c)
    yg.append(gate_up_terms(1 - c, 1))
    cx, cc = x_gather(1, cz)
    eg = [y_sum(0, 0, yg[0][0]), y_sum(1, 0, yg[0][1])]
    pass_on(1, cx, cc)
    loads[4].wait()
    eg.append(y_sum(0, 1, yg[1][0]))
    received(cc)
    ys = []
    for t in range(2):
        lay_out(1, t)
        ys.append(slope_terms(t))
    eg.append(y_sum(1, 1, yg[1][1]))
    es = [y_sum(2, t, ys[t]) for t in range(2)]

    @pl.loop(0, CHUNKS)
    def _(j):
        at = pl.ds(pl.multiple_of(j * LANES, LANES), LANES)
        acts_t[at, :] = xall[0, :, :, :, at].reshape(2 * HALF, LANES).T

    received(eg[0:2])
    yh = hidden_units(c, 0)
    received(eg[2:4])
    yh += hidden_units(1 - c, 1)
    received(es[0:1])
    yl = [slope_pair(0)]
    received(yh)
    for t in range(2):
        outputs(t)
        scatter_core(0, t)
    for t in range(2):
        scatter_x(0, t)
    received(es[1:2])
    yl.append(slope_pair(1))

    @pl.loop(0, HID // LANES)
    def _(j):
        at = pl.ds(pl.multiple_of(j * LANES, LANES), LANES)
        gradd[at, :] = over_tokens(hid[:, :, :, at], xall[1])

    write(4, gradd, dg_hbm)
    received(yl[0])
    input_slopes(0)
    scatter_core(1, 0)
    scatter_x(1, 0)
    fz_o = scatter_z(0)
    received(yl[1])
    input_slopes(1)
    scatter_core(1, 1)
    scatter_x(1, 1)

    @pl.loop(0, CHUNKS // 2)
    def _(j):
        at = pl.ds(pl.multiple_of(j * 2 * LANES, 2 * LANES), 2 * LANES)
        grads = dot(acts_t[at, :], slope[...].reshape(2 * HALF, 2 * HID), ((1,), (0,)))
        gradg[at, :] = grads[:, 0:HID].astype(BF16)
        gradu[at, :] = grads[:, HID : 2 * HID].astype(BF16)

    write(2, gradg, gg_hbm)
    write(3, gradu, ug_hbm)
    fz_i = scatter_z(1)
    finish(0, fz_o)
    finish(1, fz_i)
    for k in range(2):
        core_copy(k).wait_send()
        for order in range(2):
            for i in range(NX - 1):
                x_copy(k, order, i).wait_send()
    for copy in started:
        copy.wait_send()
    for copy in stores:
        copy.wait()


def store(*refs):
    given, results, held = refs[0:5], refs[5:10], refs[10:15]
    sems = refs[15]
    copies = []
    for i in range(5):
        copies.append(
            (
                pltpu.make_async_copy(given[i], held[i], sems.at[0, i]),
                pltpu.make_async_copy(held[i], results[i], sems.at[1, i]),
            )
        )
        copies[i][0].start()
    for read, write in copies:
        read.wait()
        write.start()
    for _, write in copies:
        write.wait()


def body(activations, gate_weight, up_weight, down_weight, output_cotangent):
    hbm = pl.BlockSpec(memory_space=pltpu.HBM)
    dma = pltpu.SemaphoreType.DMA
    small = jax.ShapeDtypeStruct((OWN, WIDTH), BF16)
    tall = jax.ShapeDtypeStruct((WIDTH, HID), BF16)
    scratch = [
        pltpu.VMEM((2, OWN, WIDTH), BF16),
        pltpu.VMEM((WIDTH, 2 * HID), BF16),
        pltpu.VMEM((HID, WIDTH), BF16),
        pltpu.VMEM((WIDTH, 2 * HALF), BF16),
        pltpu.VMEM((2, 2, NX, NZ, OWN * CHUNKS, LANES), BF16),
        pltpu.VMEM((2, 2, NX, BLOCK, WIDTH), BF16),
        pltpu.VMEM((3, 2, NY, BLOCK, HID), BF16),
        pltpu.VMEM((3, 2, NY - 1, BLOCK, HID), BF16),
        pltpu.VMEM((3, 2, BLOCK, HID), BF16),
        pltpu.VMEM((3, 2, BLOCK, HID), BF16),
        pltpu.VMEM((2, 2, BLOCK, HID), F32),
        pltpu.VMEM((2, NY, BLOCK, HID), BF16),
        pltpu.VMEM((2, NY, BLOCK, 2 * HID), BF16),
        pltpu.VMEM((2, 2, NX, BLOCK, WIDTH), BF16),
        pltpu.VMEM((2, NX, BLOCK, WIDTH), BF16),
        pltpu.VMEM((2, NX, NZ, OWN * CHUNKS, LANES), BF16),
        pltpu.VMEM((2, NX - 1, NZ, OWN * CHUNKS, LANES), BF16),
        pltpu.VMEM((2, NZ, OWN * CHUNKS, LANES), BF16),
        pltpu.VMEM((2, NZ - 1, OWN * CHUNKS, LANES), BF16),
        pltpu.VMEM((2, OWN, WIDTH), BF16),
        pltpu.VMEM((WIDTH, HID), BF16),
        pltpu.VMEM((WIDTH, HID), BF16),
        pltpu.VMEM((HID, WIDTH), BF16),
        dma((5,)),
        dma((5,)),
    ]
    for shape in (
        (2, NZ - 1), (2, 2, NX - 1), (2, 2, NX), (3, 2, NY - 1), (3, 2),
        (2, NY - 1), (2, NY - 1), (2,), (2, 2, NX - 1), (2, NZ - 1),
    ):
        scratch += [dma(shape), dma(shape)]
    shapes = (small, small, tall, tall, jax.ShapeDtypeStruct((HID, WIDTH), BF16))
    results = pl.pallas_call(
        kernel,
        out_shape=shapes,
        in_specs=[hbm] * 5,
        out_specs=(hbm,) * 5,
        scratch_shapes=scratch,
        compiler_params=pltpu.CompilerParams(
            collective_id=0, has_side_effects=True, vmem_limit_bytes=61 << 20
        ),
    )(activations, output_cotangent, gate_weight, up_weight, down_weight)
    return pl.pallas_call(
        store,
        out_shape=shapes,
        in_specs=[hbm] * 5,
        out_specs=(hbm,) * 5,
        scratch_shapes=[pltpu.VMEM(s.shape, s.dtype) for s in shapes] + [dma((2, 5))],
    )(*results)


def solution(mesh):
    in_specs = (
        P(("dp", "col"), "row"),
        P("row", ("dp", "col")),
        P("row", ("dp", "col")),
        P(("dp", "col"), "row"),
        P(("dp", "col"), "row"),
    )
    out_specs = (
        P(("dp", "col"), "row"),
        P(("dp", "col"), "row"),
        P("row", ("dp", "col")),
        P("row", ("dp", "col")),
        P(("dp", "col"), "row"),
    )
    return jax.shard_map(body, mesh=mesh, in_specs=in_specs, out_specs=out_specs, check_vma=False)
```

time: 89.2 us -> 79.8 us (0.89)
  Pallas kernels: 88.2 us -> 78.8 us
    pallas_call x1, Pallas kernels: 85.6 us -> 76.2 us  [body(): pl.pallas_call(kernel, out_shape=shapes, in_specs=[hbm] * 5, out_specs=(h...]
where the time goes in v3:
time: 79.8 us; the launch traced here: 79.5 us
  Pallas kernels  78.8 us (99%)
    pallas_call x1, Pallas kernels, body(): pl.pallas_call(kernel, out_shape=shapes, in_specs=[hbm] * 5, out_specs=(h...  76.2 us
    pallas_call x1, Pallas kernels, body(): pl.pallas_call(store, out_shape=shapes, in_specs=[hbm] * 5, out_specs=(hb...  2.65 us

profile of v3, /device:TPU:1, one launch (start us, length us, event | category | flops | bytes accessed | tf_op | source)
XLA Modules:
  0.0 79.5 jit_solution(1948025679002605483)
XLA Ops:
  0.6 76.2 %shard_map.92 = (bf16[6,1024]{1,0:T(8,128)(2,1)}, bf16[6,1024]{1,0:T(8,128)(2,1)}, bf16[1024,384]{1,0:T(8,128)(2,1)}, bf16[1024,384]{1,0:T(8,128)(2,1)}, bf16[384,1024]{1,0:T(8,128)(2,1)}) custom-call(bf16[6,1024]{1,0:T(8,128)(2,1)} %act_hbm.1, bf16[6,1024]{1,0:T(8,128)(2,1)} %cot_hbm.1, bf16[1024,384]{1,0:T(8,128)(2,1)} %gw_hbm.1, ...), custom_call_target="tpu_custom_call" | custom-call | tf_op jit(solution)/shard_map/pallas_call | solution.py:411
  76.8 2.7 %shard_map.93 = (bf16[6,1024]{1,0:T(8,128)(2,1)}, bf16[6,1024]{1,0:T(8,128)(2,1)}, bf16[1024,384]{1,0:T(8,128)(2,1)}, bf16[1024,384]{1,0:T(8,128)(2,1)}, bf16[384,1024]{1,0:T(8,128)(2,1)}) custom-call(bf16[6,1024]{1,0:T(8,128)(2,1)} %get-tuple-element.10.refs_0_, bf16[6,1024]{1,0:T(8,128)(2,1)} %get-tuple-element.11.refs_1_, ...), custom_call_target="tpu_custom_call" | custom-call | tf_op jit(solution)/shard_map/pallas_call | solution.py:421

commit v4 on v3

--- a/solution.py
+++ b/solution.py
@@ -69,6 +69,13 @@
     def zdev(m):
         return {"col": zpos(m)}
 
+    barrier = pltpu.get_barrier_semaphore()
+    peers = [far] + [zdev(m) for m in range(NZ - 1, 0, -1)]
+    peers += [ydev(i) for i in range(1, NY)]
+    peers += [xdev(i) for i in range(1, NX)] + [sib]
+    for peer in peers:
+        pl.semaphore_signal(barrier, inc=1, device_id=peer, device_id_type=MESH)
+
     loads = [
         pltpu.make_async_copy(act_hbm, mine.at[0], wsem.at[3]),
         pltpu.make_async_copy(cot_hbm, mine.at[1], wsem.at[4]),
@@ -76,16 +83,8 @@
         pltpu.make_async_copy(uw_hbm, wgu.at[:, HID : 2 * HID], wsem.at[1]),
         pltpu.make_async_copy(dw_hbm, wd, wsem.at[2]),
     ]
-    for load in loads:
+    for load in loads[0:2]:
         load.start()
-
-    barrier = pltpu.get_barrier_semaphore()
-    peers = [sib, far]
-    peers += [xdev(i) for i in range(1, NX)]
-    peers += [ydev(i) for i in range(1, NY)]
-    peers += [zdev(m) for m in range(1, NZ)]
-    for peer in peers:
-        pl.semaphore_signal(barrier, inc=1, device_id=peer, device_id_type=MESH)
 
     def to_fine(value):
         return value.reshape(value.shape[0] * CHUNKS, LANES)
@@ -112,7 +111,7 @@
     def z_gather(kind):
         piece = xfine.at[kind, c, x, zl]
         copies = {}
-        for m in (7, 6, 5, 4, 3, 2, 1):
+        for m in (1, 2, 3, 4, 5, 6, 7):
             copies[m] = send(piece, piece, z_s.at[kind, m - 1], z_r.at[kind, m - 1], zdev(m))
         return copies
 
@@ -132,16 +131,24 @@
             cs.append(forward(kind, x, order, 0))
         return xs, cs
 
+    def lay_out(kind, t, where):
+        pieces = xfine[kind, t, where].reshape(BLOCK * CHUNKS, LANES)
+        xall[kind, t, where] = from_fine(pieces.astype(F32)).astype(BF16)
+
     def pass_on(kind, xs, cs):
+        lay_out(kind, c, x)
         for order in range(2):
             for i in (0, 2, 1):
+                where = lax.rem(x + NX - i - 1, NX)
                 xs[order * (NX - 1) + i].wait_recv()
-                cs.append(forward(kind, lax.rem(x + NX - i - 1, NX), order, i + 1))
-
-    def lay_out(kind, t):
+                cs.append(forward(kind, where, order, i + 1))
+                if order == 1:
+                    lay_out(kind, c, where)
+
+    def from_sibling(kind, cs):
+        received(cs)
         for where in range(NX):
-            pieces = xfine[kind, t, where].reshape(BLOCK * CHUNKS, LANES)
-            xall[kind, t, where] = from_fine(pieces.astype(F32)).astype(BF16)
+            lay_out(kind, 1 - c, where)
 
     def y_scatter(q, k):
         return [
@@ -179,10 +186,11 @@
         for copy in copies:
             copy.wait_recv()
 
-    def core_copy(k):
+    def core_copy(k, i):
+        where = xpos(i)
         return pltpu.make_async_remote_copy(
-            src_ref=part.at[k, 1 - c], dst_ref=crecv.at[k], send_sem=fc_s.at[k],
-            recv_sem=fc_r.at[k], device_id=sib, device_id_type=MESH,
+            src_ref=part.at[k, 1 - c, where], dst_ref=crecv.at[k, where], send_sem=fc_s.at[k, i],
+            recv_sem=fc_r.at[k, i], device_id=sib, device_id_type=MESH,
         )
 
     def x_copy(k, order, i):
@@ -196,18 +204,20 @@
     def scatter_core(k, t):
         @pl.when(c == 1 - t)
         def _():
-            core_copy(k).start()
+            for i in (2, 1, 3, 0):
+                core_copy(k, i).start()
 
     def scatter_x(k, t):
         @pl.when(c == t)
         def _():
-            core_copy(k).wait_recv()
-            for where in range(NX):
+            for i in (2, 1, 3, 0):
+                where = xpos(i)
+                core_copy(k, i).wait_recv()
                 total = part[k, c, where].astype(F32) + crecv[k, where].astype(F32)
                 xsend[k, where] = to_fine(total).astype(BF16).reshape(NZ, OWN * CHUNKS, LANES)
-            for order in range(2):
-                for i in range(NX - 1):
-                    x_copy(k, order, i).start()
+                if i > 0:
+                    for order in range(2):
+                        x_copy(k, order, i - 1).start()
 
     def scatter_z(k):
         copies = []
@@ -269,33 +279,34 @@
         part[1, t] = total.astype(BF16).reshape(NX, BLOCK, WIDTH)
 
     az = z_gather(0)
+    for load in loads[2:5]:
+        load.start()
     ax, ac = x_gather(0, az)
     cz = z_gather(1)
     pass_on(0, ax, ac)
-    lay_out(0, c)
     loads[2].wait()
     loads[3].wait()
     yg = [gate_up_terms(c, 0)]
-    received(ac)
-    lay_out(0, 1 - c)
+    from_sibling(0, ac)
     yg.append(gate_up_terms(1 - c, 1))
     cx, cc = x_gather(1, cz)
     eg = [y_sum(0, 0, yg[0][0]), y_sum(1, 0, yg[0][1])]
     pass_on(1, cx, cc)
     loads[4].wait()
     eg.append(y_sum(0, 1, yg[1][0]))
-    received(cc)
-    ys = []
-    for t in range(2):
-        lay_out(1, t)
-        ys.append(slope_terms(t))
+    from_sibling(1, cc)
+    ys = [slope_terms(t) for t in range(2)]
     eg.append(y_sum(1, 1, yg[1][1]))
+    gathers = [copy for copy in started if all(copy is not other for other in eg)]
     es = [y_sum(2, t, ys[t]) for t in range(2)]
 
     @pl.loop(0, CHUNKS)
     def _(j):
         at = pl.ds(pl.multiple_of(j * LANES, LANES), LANES)
         acts_t[at, :] = xall[0, :, :, :, at].reshape(2 * HALF, LANES).T
+
+    for copy in gathers:
+        copy.wait_send()
 
     received(eg[0:2])
     yh = hidden_units(c, 0)
@@ -341,12 +352,14 @@
     finish(0, fz_o)
     finish(1, fz_i)
     for k in range(2):
-        core_copy(k).wait_send()
+        for i in range(NX):
+            core_copy(k, i).wait_send()
         for order in range(2):
             for i in range(NX - 1):
                 x_copy(k, order, i).wait_send()
     for copy in started:
-        copy.wait_send()
+        if all(copy is not other for other in gathers):
+            copy.wait_send()
     for copy in stores:
         copy.wait()
 
@@ -404,7 +417,7 @@
     ]
     for shape in (
         (2, NZ - 1), (2, 2, NX - 1), (2, 2, NX), (3, 2, NY - 1), (3, 2),
-        (2, NY - 1), (2, NY - 1), (2,), (2, 2, NX - 1), (2, NZ - 1),
+        (2, NY - 1), (2, NY - 1), (2, NX), (2, 2, NX - 1), (2, NZ - 1),
     ):
         scratch += [dma(shape), dma(shape)]
     shapes = (small, small, tall, tall, jax.ShapeDtypeStruct((HID, WIDTH), BF16))

time: 79.8 us -> 79.8 us (level)
  no operation moved by 1% of the time
where the time goes in v4:
time: 79.8 us; the launch traced here: 79.4 us
  Pallas kernels  78.8 us (99%)
    pallas_call x1, Pallas kernels, body(): pl.pallas_call(kernel, out_shape=shapes, in_specs=[hbm] * 5, out_specs=(h...  76.1 us
    pallas_call x1, Pallas kernels, body(): pl.pallas_call(store, out_shape=shapes, in_specs=[hbm] * 5, out_specs=(hb...  2.65 us

profile of v4, /device:TPU:1, one launch (start us, length us, event | category | flops | bytes accessed | tf_op | source)
XLA Modules:
  0.0 79.4 jit_solution(12662806938599485678)
XLA Ops:
  0.6 76.1 %shard_map.92 = (bf16[6,1024]{1,0:T(8,128)(2,1)}, bf16[6,1024]{1,0:T(8,128)(2,1)}, bf16[1024,384]{1,0:T(8,128)(2,1)}, bf16[1024,384]{1,0:T(8,128)(2,1)}, bf16[384,1024]{1,0:T(8,128)(2,1)}) custom-call(bf16[6,1024]{1,0:T(8,128)(2,1)} %act_hbm.1, bf16[6,1024]{1,0:T(8,128)(2,1)} %cot_hbm.1, bf16[1024,384]{1,0:T(8,128)(2,1)} %gw_hbm.1, ...), custom_call_target="tpu_custom_call" | custom-call | tf_op jit(solution)/shard_map/pallas_call | solution.py:424
  76.7 2.7 %shard_map.93 = (bf16[6,1024]{1,0:T(8,128)(2,1)}, bf16[6,1024]{1,0:T(8,128)(2,1)}, bf16[1024,384]{1,0:T(8,128)(2,1)}, bf16[1024,384]{1,0:T(8,128)(2,1)}, bf16[384,1024]{1,0:T(8,128)(2,1)}) custom-call(bf16[6,1024]{1,0:T(8,128)(2,1)} %get-tuple-element.10.refs_0_, bf16[6,1024]{1,0:T(8,128)(2,1)} %get-tuple-element.11.refs_1_, ...), custom_call_target="tpu_custom_call" | custom-call | tf_op jit(solution)/shard_map/pallas_call | solution.py:434

commit v5 on v4

--- a/solution.py
+++ b/solution.py
@@ -111,7 +111,7 @@
     def z_gather(kind):
         piece = xfine.at[kind, c, x, zl]
         copies = {}
-        for m in (1, 2, 3, 4, 5, 6, 7):
+        for m in (7, 6, 5, 4, 3, 2, 1):
             copies[m] = send(piece, piece, z_s.at[kind, m - 1], z_r.at[kind, m - 1], zdev(m))
         return copies
 
@@ -339,6 +339,8 @@
     scatter_core(1, 1)
     scatter_x(1, 1)
 
+    fz_i = scatter_z(1)
+
     @pl.loop(0, CHUNKS // 2)
     def _(j):
         at = pl.ds(pl.multiple_of(j * 2 * LANES, 2 * LANES), 2 * LANES)
@@ -348,9 +350,7 @@
 
     write(2, gradg, gg_hbm)
     write(3, gradu, ug_hbm)
-    fz_i = scatter_z(1)
     finish(0, fz_o)
-    finish(1, fz_i)
     for k in range(2):
         for i in range(NX):
             core_copy(k, i).wait_send()
@@ -360,6 +360,7 @@
     for copy in started:
         if all(copy is not other for other in gathers):
             copy.wait_send()
+    finish(1, fz_i)
     for copy in stores:
         copy.wait()
 

time: 79.8 us -> 78.7 us (0.986)
  Pallas kernels: 78.8 us -> 77.7 us
    pallas_call x1, Pallas kernels: 76.1 us -> 75 us  [body(): pl.pallas_call(kernel, out_shape=shapes, in_specs=[hbm] * 5, out_specs=(h...]
where the time goes in v5:
time: 78.7 us; the launch traced here: 78.3 us
  Pallas kernels  77.7 us (99%)
    pallas_call x1, Pallas kernels, body(): pl.pallas_call(kernel, out_shape=shapes, in_specs=[hbm] * 5, out_specs=(h...  75 us
    pallas_call x1, Pallas kernels, body(): pl.pallas_call(store, out_shape=shapes, in_specs=[hbm] * 5, out_specs=(hb...  2.65 us

profile of v5, /device:TPU:1, one launch (start us, length us, event | category | flops | bytes accessed | tf_op | source)
XLA Modules:
  0.0 78.3 jit_solution(14384061637112837769)
XLA Ops:
  0.6 75.0 %shard_map.92 = (bf16[6,1024]{1,0:T(8,128)(2,1)}, bf16[6,1024]{1,0:T(8,128)(2,1)}, bf16[1024,384]{1,0:T(8,128)(2,1)}, bf16[1024,384]{1,0:T(8,128)(2,1)}, bf16[384,1024]{1,0:T(8,128)(2,1)}) custom-call(bf16[6,1024]{1,0:T(8,128)(2,1)} %act_hbm.1, bf16[6,1024]{1,0:T(8,128)(2,1)} %cot_hbm.1, bf16[1024,384]{1,0:T(8,128)(2,1)} %gw_hbm.1, ...), custom_call_target="tpu_custom_call" | custom-call | tf_op jit(solution)/shard_map/pallas_call | solution.py:425
  75.7 2.7 %shard_map.93 = (bf16[6,1024]{1,0:T(8,128)(2,1)}, bf16[6,1024]{1,0:T(8,128)(2,1)}, bf16[1024,384]{1,0:T(8,128)(2,1)}, bf16[1024,384]{1,0:T(8,128)(2,1)}, bf16[384,1024]{1,0:T(8,128)(2,1)}) custom-call(bf16[6,1024]{1,0:T(8,128)(2,1)} %get-tuple-element.10.refs_0_, bf16[6,1024]{1,0:T(8,128)(2,1)} %get-tuple-element.11.refs_1_, ...), custom_call_target="tpu_custom_call" | custom-call | tf_op jit(solution)/shard_map/pallas_call | solution.py:435
